TPU v7x, 32 devices: a whole 2x2x4 slice. The times are simulated.
32 devices in a mesh: seq: 16 (over z, x, core), fsdp: 2 (over y).
Axes of the slice: x: 2, y: 2, z: 4, core: 2. Of those that a mesh axis runs over, the one named last changes fastest.
Arguments:
- tokens: bfloat16 [112, 56, 384], P('seq', 'fsdp'), may hold values from -6 to 6
- norm_gains: bfloat16 [2, 2, 384], P(None, None, 'fsdp'), may hold values from 0.25 to 1.75
- w_qkv: bfloat16 [2, 384, 1152], P(None, 'fsdp'), may hold values from -0.3125 to 0.3125
- w_proj: bfloat16 [2, 384, 384], P(None, 'fsdp'), may hold values from -0.875 to 0.875
- w_up: bfloat16 [2, 384, 1536], P(None, 'fsdp'), may hold values from -0.3125 to 0.3125
- w_down: bfloat16 [2, 1536, 384], P(None, 'fsdp'), may hold values from -0.15625 to 0.15625
- tables: bfloat16 [2, 12, 169], P(None, 'fsdp'), may hold values from -4 to 4
- region_ids: int32 [112, 56], P('seq', 'fsdp'), may hold values from 0 to 3, as said below
- rel_index: int32 [49, 49], replicated, may hold values from 0 to 168, as said below
- cotangent: bfloat16 [112, 56, 384], P('seq', 'fsdp'), may hold values from -6 to 6
Outputs:
- mixed: bfloat16 [112, 56, 384], P('seq', 'fsdp')
- tokens_grad: bfloat16 [112, 56, 384], P('seq', 'fsdp')
- gains_grad: float32 [2, 2, 384], P(None, None, 'fsdp')
- qkv_grad: float32 [2, 384, 1152], P(None, 'fsdp')
- proj_grad: float32 [2, 384, 384], P(None, 'fsdp')
- up_grad: float32 [2, 384, 1536], P(None, 'fsdp')
- down_grad: float32 [2, 1536, 384], P(None, 'fsdp')
- tables_grad: float32 [2, 12, 169], P(None, 'fsdp')
Inputs may be any that keep to these rules, and one draw needn't show every extreme that they name: `region_ids`: labels of the tokens of the grid rolled by -3; inside a window, tokens attend only to tokens of the same label. `rel_index`: entry (i, j) depends only on the offset between positions i and j of a window (row-major) and differs for different offsets.
All inputs are finite; a program needn't handle non-finite values.
Results may differ from a plain program's by a relative error of at most 0.02.
Values may be sent and summed in bfloat16 or wider, within the bound.
No kernel may reach another device: no remote copies, remote signals or barrier semaphores. Data moves between devices by JAX's collectives and lax.ppermute only.
A program may use at most 128 MiB of HBM per device.

v0:
```python
import jax
import jax.numpy as jnp
from jax import lax
from jax.sharding import PartitionSpec as P

WIN = 7
SHIFT = 3
TABLE = 169


EPSILON = 1e-05
MASKED_SCORE = -1000000000.0


def from_behind(array, axis, by):
    count = lax.axis_size(axis)
    return lax.ppermute(array, axis, [(i, (i + by) % count) for i in range(count)])


def to_windows(band):
    rows, width, feat = band.shape
    split = band.reshape(rows, width // WIN, WIN, feat)
    return split.transpose(1, 0, 2, 3).reshape(-1, feat)


def from_windows(flat, width):
    feat = flat.shape[-1]
    split = flat.reshape(width // WIN, WIN, WIN, feat)
    return split.transpose(1, 0, 2, 3).reshape(WIN, width, feat)


def roll_in(band):
    below = from_behind(band[:SHIFT], "seq", -1)
    tall = jnp.concatenate([band[SHIFT:], below], axis=0)
    beside = from_behind(tall[:, :SHIFT], "fsdp", -1)
    return jnp.concatenate([tall[:, SHIFT:], beside], axis=1)


def roll_out(band):
    width = band.shape[1]
    before = from_behind(band[:, width - SHIFT :], "fsdp", 1)
    wide = jnp.concatenate([before, band[:, : width - SHIFT]], axis=1)
    above = from_behind(wide[WIN - SHIFT :], "seq", 1)
    return jnp.concatenate([above, wide[: WIN - SHIFT]], axis=0)


def normalize(values):
    centred = values - jnp.mean(values, -1, keepdims=True)
    factor = lax.rsqrt(jnp.mean(centred * centred, -1, keepdims=True) + EPSILON)
    return (centred * factor, factor)


def normalize_back(grad_norm, normed, factor):
    spread = jnp.mean(grad_norm * normed, -1, keepdims=True)
    return factor * (grad_norm - jnp.mean(grad_norm, -1, keepdims=True) - normed * spread)


def attend_scores(query, keys, bias, labels):
    raw = jnp.einsum("wihd,wjhd->whij", query, keys, preferred_element_type=jnp.float32)
    scores = raw + bias[None]
    if labels is None:
        return scores
    same = labels[:, :, None] == labels[:, None, :]
    return jnp.where(same[:, None], scores, MASKED_SCORE)


def layer_forward(flat, params, labels, onehot):
    gains, qkv_w, proj_w, up_w, down_w, table = params
    count, width_c = flat.shape
    nwin = count // (WIN * WIN)
    heads = table.shape[0]
    head = width_c // heads
    bias = jnp.dot(table.astype(jnp.float32), onehot.T, precision=lax.Precision.HIGHEST).reshape(
        heads, WIN * WIN, WIN * WIN
    )
    normed_a, factor_a = normalize(flat)
    hidden_q = (normed_a * gains[0].astype(jnp.float32)).astype(jnp.bfloat16)
    qkv = jnp.dot(hidden_q, qkv_w, preferred_element_type=jnp.float32)
    shape_h = (nwin, WIN * WIN, heads, head)
    query = (qkv[:, :width_c] * head ** (-0.5)).astype(jnp.bfloat16).reshape(shape_h)
    keys = qkv[:, width_c : 2 * width_c].astype(jnp.bfloat16).reshape(shape_h)
    values = qkv[:, 2 * width_c :].astype(jnp.bfloat16).reshape(shape_h)
    scores = attend_scores(query, keys, bias, labels)
    highest = jnp.max(scores, -1, keepdims=True)
    weighted = jnp.exp(scores - highest)
    total = jnp.sum(weighted, -1, keepdims=True)
    attention = weighted / total
    logsum = highest + jnp.log(total)
    mixed = jnp.einsum(
        "whij,wjhd->wihd",
        attention.astype(jnp.bfloat16),
        values,
        preferred_element_type=jnp.float32,
    )
    mixed = mixed.reshape(count, width_c).astype(jnp.bfloat16)
    middle = flat + jnp.dot(mixed, proj_w, preferred_element_type=jnp.float32)
    normed_b, factor_b = normalize(middle)
    hidden_b = (normed_b * gains[1].astype(jnp.float32)).astype(jnp.bfloat16)
    inner = jnp.dot(hidden_b, up_w, preferred_element_type=jnp.float32)
    activated = jax.nn.gelu(inner).astype(jnp.bfloat16)
    output = middle + jnp.dot(activated, down_w, preferred_element_type=jnp.float32)
    kept = (
        hidden_q,
        query,
        keys,
        values,
        logsum,
        mixed,
        normed_a,
        factor_a,
        normed_b,
        factor_b,
        hidden_b,
        inner,
        activated,
        bias,
    )
    return (output, kept)


def layer_backward(grad_out, params, kept, labels, onehot):
    gains, qkv_w, proj_w, up_w, down_w, table = params
    (
        hidden_q,
        query,
        keys,
        values,
        logsum,
        mixed,
        normed_a,
        factor_a,
        normed_b,
        factor_b,
        hidden_b,
        inner,
        activated,
        bias,
    ) = kept
    count, width_c = grad_out.shape
    heads = table.shape[0]
    head = width_c // heads
    grad_low = grad_out.astype(jnp.bfloat16)
    down_grad = jnp.dot(activated.T, grad_low, preferred_element_type=jnp.float32)
    grad_act = jnp.dot(grad_low, down_w.T, preferred_element_type=jnp.float32)
    gelu_pull = jax.vjp(jax.nn.gelu, inner)[1]
    grad_inner = gelu_pull(grad_act)[0].astype(jnp.bfloat16)
    up_grad = jnp.dot(hidden_b.T, grad_inner, preferred_element_type=jnp.float32)
    grad_hidden_b = jnp.dot(grad_inner, up_w.T, preferred_element_type=jnp.float32)
    gain_b_grad = jnp.sum(grad_hidden_b * normed_b, 0)
    grad_middle = grad_out + normalize_back(
        grad_hidden_b * gains[1].astype(jnp.float32), normed_b, factor_b
    )
    grad_attended = grad_middle.astype(jnp.bfloat16)
    proj_grad = jnp.dot(mixed.T, grad_attended, preferred_element_type=jnp.float32)
    grad_mixed = jnp.dot(grad_attended, proj_w.T, preferred_element_type=jnp.float32).astype(
        jnp.bfloat16
    )
    grad_mixed = grad_mixed.reshape(query.shape)
    scores = attend_scores(query, keys, bias, labels)
    attention = jnp.exp(scores - logsum)
    grad_values = jnp.einsum(
        "whij,wihd->wjhd",
        attention.astype(jnp.bfloat16),
        grad_mixed,
        preferred_element_type=jnp.float32,
    )
    grad_attention = jnp.einsum(
        "wihd,wjhd->whij", grad_mixed, values, preferred_element_type=jnp.float32
    )
    grad_scores = attention * (
        grad_attention - jnp.sum(grad_attention * attention, -1, keepdims=True)
    )
    grad_bias = jnp.sum(grad_scores, 0).reshape(heads, -1)
    table_grad = jnp.dot(grad_bias, onehot, precision=lax.Precision.HIGHEST)
    grad_raw = grad_scores.astype(jnp.bfloat16)
    grad_query = jnp.einsum(
        "whij,wjhd->wihd", grad_raw, keys, preferred_element_type=jnp.float32
    ) * head ** (-0.5)
    grad_keys = jnp.einsum("whij,wihd->wjhd", grad_raw, query, preferred_element_type=jnp.float32)
    grad_qkv = jnp.concatenate(
        [
            grad_query.reshape(count, width_c),
            grad_keys.reshape(count, width_c),
            grad_values.reshape(count, width_c),
        ],
        axis=1,
    ).astype(jnp.bfloat16)
    qkv_grad = jnp.dot(hidden_q.T, grad_qkv, preferred_element_type=jnp.float32)
    grad_hidden_q = jnp.dot(grad_qkv, qkv_w.T, preferred_element_type=jnp.float32)
    gain_a_grad = jnp.sum(grad_hidden_q * normed_a, 0)
    grad_input = grad_middle + normalize_back(
        grad_hidden_q * gains[0].astype(jnp.float32), normed_a, factor_a
    )
    return (
        grad_input,
        (
            jnp.stack([gain_a_grad, gain_b_grad]),
            qkv_grad,
            proj_grad,
            up_grad,
            down_grad,
            table_grad,
        ),
    )


def per_device(
    tokens, norm_gains, w_qkv, w_proj, w_up, w_down, tables, region_ids, rel_index, cotangent
):
    gathered = (
        lax.all_gather(norm_gains, "fsdp", axis=2, tiled=True),
        lax.all_gather(w_qkv, "fsdp", axis=1, tiled=True),
        lax.all_gather(w_proj, "fsdp", axis=1, tiled=True),
        lax.all_gather(w_up, "fsdp", axis=1, tiled=True),
        lax.all_gather(w_down, "fsdp", axis=1, tiled=True),
        lax.all_gather(tables, "fsdp", axis=1, tiled=True),
    )
    params_one = tuple((item[0] for item in gathered))
    params_two = tuple((item[1] for item in gathered))
    onehot = (rel_index.reshape(-1)[:, None] == jnp.arange(TABLE, dtype=jnp.int32)[None, :]).astype(
        jnp.float32
    )
    width = tokens.shape[1]
    labels = to_windows(region_ids[:, :, None]).reshape(-1, WIN * WIN)
    output_one, kept_one = layer_forward(
        to_windows(tokens.astype(jnp.float32)), params_one, None, onehot
    )
    middle = from_windows(output_one, width).astype(jnp.bfloat16)
    rolled = roll_in(middle)
    output_two, kept_two = layer_forward(
        to_windows(rolled.astype(jnp.float32)), params_two, labels, onehot
    )
    mixed = roll_out(from_windows(output_two, width).astype(jnp.bfloat16))
    grad_top = to_windows(roll_in(cotangent).astype(jnp.float32))
    grad_mid, grads_two = layer_backward(grad_top, params_two, kept_two, labels, onehot)
    grad_back = roll_out(from_windows(grad_mid, width).astype(jnp.bfloat16))
    grad_input, grads_one = layer_backward(
        to_windows(grad_back.astype(jnp.float32)), params_one, kept_one, None, onehot
    )
    tokens_grad = from_windows(grad_input, width).astype(jnp.bfloat16)
    shards = (
        lax.psum_scatter(
            grads_one[0].astype(jnp.bfloat16), "fsdp", scatter_dimension=1, tiled=True
        ).astype(jnp.float32),
        lax.psum_scatter(
            grads_one[1].astype(jnp.bfloat16), "fsdp", scatter_dimension=0, tiled=True
        ).astype(jnp.float32),
        lax.psum_scatter(
            grads_one[2].astype(jnp.bfloat16), "fsdp", scatter_dimension=0, tiled=True
        ).astype(jnp.float32),
        lax.psum_scatter(
            grads_one[3].astype(jnp.bfloat16), "fsdp", scatter_dimension=0, tiled=True
        ).astype(jnp.float32),
        lax.psum_scatter(
            grads_one[4].astype(jnp.bfloat16), "fsdp", scatter_dimension=0, tiled=True
        ).astype(jnp.float32),
        lax.psum_scatter(
            grads_one[5].astype(jnp.bfloat16), "fsdp", scatter_dimension=0, tiled=True
        ).astype(jnp.float32),
        lax.psum_scatter(
            grads_two[0].astype(jnp.bfloat16), "fsdp", scatter_dimension=1, tiled=True
        ).astype(jnp.float32),
        lax.psum_scatter(
            grads_two[1].astype(jnp.bfloat16), "fsdp", scatter_dimension=0, tiled=True
        ).astype(jnp.float32),
        lax.psum_scatter(
            grads_two[2].astype(jnp.bfloat16), "fsdp", scatter_dimension=0, tiled=True
        ).astype(jnp.float32),
        lax.psum_scatter(
            grads_two[3].astype(jnp.bfloat16), "fsdp", scatter_dimension=0, tiled=True
        ).astype(jnp.float32),
        lax.psum_scatter(
            grads_two[4].astype(jnp.bfloat16), "fsdp", scatter_dimension=0, tiled=True
        ).astype(jnp.float32),
        lax.psum_scatter(
            grads_two[5].astype(jnp.bfloat16), "fsdp", scatter_dimension=0, tiled=True
        ).astype(jnp.float32),
    )
    summed = lax.psum(
        (
            shards[0],
            shards[1],
            shards[2],
            shards[3],
            shards[4],
            shards[5],
            shards[6],
            shards[7],
            shards[8],
            shards[9],
            shards[10],
            shards[11],
        ),
        "seq",
    )
    totals = tuple((jnp.stack([summed[index], summed[index + 6]]) for index in range(6)))
    return (mixed, tokens_grad, totals[0], totals[1], totals[2], totals[3], totals[4], totals[5])


def solution(mesh):
    return jax.shard_map(
        per_device,
        mesh=mesh,
        in_specs=(
            P("seq", "fsdp", None),
            P(None, None, "fsdp"),
            P(None, "fsdp", None),
            P(None, "fsdp", None),
            P(None, "fsdp", None),
            P(None, "fsdp", None),
            P(None, "fsdp", None),
            P("seq", "fsdp"),
            P(),
            P("seq", "fsdp", None),
        ),
        out_specs=(
            P("seq", "fsdp", None),
            P("seq", "fsdp", None),
            P(None, None, "fsdp"),
            P(None, "fsdp", None),
            P(None, "fsdp", None),
            P(None, "fsdp", None),
            P(None, "fsdp", None),
            P(None, "fsdp", None),
        ),
        check_vma=False,
    )
```

profile of v0, /device:TPU:0, one launch (start us, length us, event | category | flops | bytes accessed | tf_op | source)
XLA Modules:
  0.0 543.6 jit_solution(7766841615037768030)
XLA Ops:
  8.8 5.5 %collective-permute-start.4 = (bf16[3,28,384]{2,0,1:T(4,128)(2,1)S(1)}, bf16[3,28,384]{2,0,1:T(4,128)(2,1)S(1)}, u32[]{:S(2)}, u32[]{:S(2)}) collective-permute-start(bf16[3,28,384]{2,0,1:T(4,128)(2,1)S(1)} %copy.277), channel_id=1, source_target_pairs={{0,30},{2,0},{4,2},{6,4},{8,6},{10,8},{12,10},{14,12},{16,14},{18,... | collective-permute-start | bytes 193544 | tf_op jit(solution)/shard_map/ppermute | solution.py:17
  15.0 5.3 all_gather.18
  20.3 4.6 fusion.81
  25.1 4.5 all_gather.20
  31.3 14.8 %all_gather.21 = bf16[2,384,384]{2,1,0:T(8,128)(2,1)S(1)} all-gather(bf16[2,192,384]{2,1,0:T(8,128)(2,1)S(1)} %copy-done.47), channel_id=1, replica_groups=mesh['seq'=16,'fsdp'=2] {'fsdp'}, dimensions={1}, use_global_device_ids=true | all-gather | bytes 884736 | tf_op jit(solution)/shard_map/all_gather | solution.py:213
  49.2 1.5 collective-permute-start.5
  50.9 1.6 fusion.110
  54.5 1.6 fusion.111
  58.9 27.1 %all-gather.6.cloned.1.call-done = bf16[2,384,1536]{2,1,0:T(8,128)(2,1)} async-done(((bf16[2,192,1536]{2,1,0:T(8,128)(2,1)}), bf16[2,384,1536]{2,1,0:T(8,128)(2,1)}) %all-gather.6.cloned.1.call-update) | async-done | bytes 2359312 | tf_op jit(solution)/shard_map/all_gather | solution.py:214
  86.0 2.8 fusion.42
  88.9 34.8 %all-gather.8.cloned.1.call-done = bf16[2,1536,384]{2,1,0:T(8,128)(2,1)} async-done(((bf16[2,768,384]{2,1,0:T(8,128)(2,1)}), bf16[2,1536,384]{2,1,0:T(8,128)(2,1)}) %all-gather.8.cloned.1.call-update) | async-done | bytes 2359312 | tf_op jit(solution)/shard_map/all_gather | solution.py:215
  123.7 2.2 fusion.35
  126.0 3.9 collective-permute-start
  130.9 1.1 collective-permute-done
  132.7 3.1 collective-permute-done.1
  137.3 1.6 fusion.113
  142.4 1.8 fusion.114
  146.7 1.9 convert_element_type.301
  148.7 1.8 copy.204
  150.5 1.8 reshape.350
  152.2 1.5 fusion.115
  154.0 2.0 fusion.45
  158.1 1.2 multiply_reduce_fusion.4
  161.5 1.9 reshape.356
  163.5 2.3 fusion.32
  166.4 1.2 fusion.106
  169.2 1.3 copy.233
  176.1 2.7 multiply_reduce_fusion.5
  181.0 1.9 collective-permute-done.6
  183.1 6.5 %collective-permute-done.7 = bf16[3,28,384]{2,0,1:T(4,128)(2,1)S(1)} collective-permute-done((bf16[3,28,384]{2,0,1:T(4,128)(2,1)S(1)}, bf16[3,28,384]{2,0,1:T(4,128)(2,1)S(1)}, u32[]{:S(2)}, u32[]{:S(2)}) %collective-permute-start.7) | collective-permute-done | bytes 64544 | tf_op jit(solution)/shard_map/ppermute | solution.py:17
  189.9 2.9 fusion.17
  192.9 1.1 multiply_reduce_fusion.6
  196.4 2.7 convolution_convert_fusion.4
  201.5 2.0 reshape.365
  204.0 1.3 fusion.105
  207.8 1.5 convolution_convert_fusion.5
  209.5 1.6 convolution_convert_fusion.2
  211.2 2.6 convolution_convert_fusion
  214.9 1.6 convolution_convert_fusion.3
  216.7 3.1 convolution_convert_fusion.1
  220.8 1.7 multiply_reduce_fusion.7
  223.8 1.6 bitcast_convert_fusion.6
  225.4 1.7 bitcast_convert_fusion.7
  227.6 2.0 bitcast_convert_fusion.4
  229.6 18.8 %reduce-scatter.19.cloned.1.call-done = bf16[192,1152]{1,0:T(8,128)(2,1)} async-done(((bf16[384,1152]{1,0:T(8,128)(2,1)}), bf16[192,1152]{1,0:T(8,128)(2,1)}) %reduce-scatter.19.cloned.1.call-update) | async-done | bytes 442384 | tf_op jit(solution)/shard_map/reduce_scatter | solution.py:245
  248.4 2.0 bitcast_convert_fusion.5
  250.4 22.6 %reduce-scatter.29.cloned.1.call-done = bf16[192,1536]{1,0:T(8,128)(2,1)} async-done(((bf16[384,1536]{1,0:T(8,128)(2,1)}), bf16[192,1536]{1,0:T(8,128)(2,1)}) %reduce-scatter.29.cloned.1.call-update) | async-done | bytes 589840 | tf_op jit(solution)/shard_map/reduce_scatter | solution.py:269
  273.0 2.2 bitcast_convert_fusion.2
  275.2 21.9 %reduce-scatter.33.cloned.1.call-done = bf16[768,384]{1,0:T(8,128)(2,1)} async-done(((bf16[1536,384]{1,0:T(8,128)(2,1)}), bf16[768,384]{1,0:T(8,128)(2,1)}) %reduce-scatter.33.cloned.1.call-update) | async-done | bytes 589840 | tf_op jit(solution)/shard_map/reduce_scatter | solution.py:272
  297.1 2.2 bitcast_convert_fusion
  299.3 21.7 %reduce-scatter.27.cloned.1.call-done = bf16[192,1536]{1,0:T(8,128)(2,1)} async-done(((bf16[384,1536]{1,0:T(8,128)(2,1)}), bf16[192,1536]{1,0:T(8,128)(2,1)}) %reduce-scatter.27.cloned.1.call-update) | async-done | bytes 589840 | tf_op jit(solution)/shard_map/reduce_scatter | solution.py:251
  321.0 2.2 bitcast_convert_fusion.3
  323.2 21.9 %reduce-scatter.31.cloned.1.call-done = bf16[768,384]{1,0:T(8,128)(2,1)} async-done(((bf16[1536,384]{1,0:T(8,128)(2,1)}), bf16[768,384]{1,0:T(8,128)(2,1)}) %reduce-scatter.31.cloned.1.call-update) | async-done | bytes 589840 | tf_op jit(solution)/shard_map/reduce_scatter | solution.py:254
  345.1 2.2 bitcast_convert_fusion.1
  349.2 1.9 fusion.36
  353.7 4.2 reduce-scatter.37.cloned.1.call-done
  360.3 5.1 fusion.104
  365.4 2.1 collective-permute-start.8
  367.6 1.3 collective-permute-start.9
  371.9 63.5 %all-reduce.4 = (f32[1,2,192]{2,1,0:T(2,128)S(1)}, f32[1,2,192]{2,1,0:T(2,128)S(1)}, f32[1,6,169]{2,1,0:T(8,128)S(1)}, f32[1,6,169]{2,1,0:T(8,128)S(1)}) all-reduce(f32[1,2,192]{2,1,0:T(2,128)S(1)} %bitcast_convert_fusion.8, f32[1,2,192]{2,1,0:T(2,128)S(1)} %bitcast_convert_fusion.9, ...), channel_id=1, replica_groups=mesh['seq'=16,'fsdp'=2] {'seq'}, use_global_device_ids=true, to_apply=%region_29.30 | all-reduce | flops 2796 | bytes 22368 | tf_op jit(solution)/shard_map/psum | solution.py:279
  436.6 92.4 %all-reduce.9.cloned.1.call-done = (f32[1,192,1152]{2,1,0:T(8,128)}, f32[1,192,1152]{2,1,0:T(8,128)}, f32[1,192,384]{2,1,0:T(8,128)}, f32[1,192,384]{2,1,0:T(8,1...) async-done(((f32[1,192,1152]{2,1,0:T(8,128)}, f32[1,192,1152]{2,1,0:T(8,128)}, ...) | async-done | bytes 7077904 | tf_op jit(solution)/shard_map/psum | solution.py:279
  528.9 3.3 pad_maximum_fusion.1
  532.3 1.6 pad_maximum_fusion
  535.3 1.3 pad_maximum_fusion.2
  (405 shorter events, 58.8 us)
Async XLA Ops:
  7.2 43.7 %all-gather.4.cloned.1.call-start = ((), (), s32[]{:S(2)}) async-start(), calls=%async_computation.10 | async-start | bytes 2654208 | tf_op jit(solution)/shard_map/all_gather | solution.py:212
  7.9 6.5 %copy-start.54 = (bf16[7,28,384]{2,1,0:T(8,128)(2,1)S(1)}, bf16[7,28,384]{2,1,0:T(8,128)(2,1)}, u32[]{:S(2)}) copy-start(bf16[7,28,384]{2,1,0:T(8,128)(2,1)} %param.10) | copy-start | bytes 451588
  7.9 78.1 %all-gather.6.cloned.1.call-start = ((), (), s32[]{:S(2)}) async-start(), calls=%async_computation.11 | async-start | bytes 3538944 | tf_op jit(solution)/shard_map/all_gather | solution.py:214
  8.7 115.0 %all-gather.8.cloned.1.call-start = ((), (), s32[]{:S(2)}) async-start(), calls=%async_computation.12 | async-start | bytes 3538944 | tf_op jit(solution)/shard_map/all_gather | solution.py:215
  8.8 6.1 %copy-start.84 = (bf16[2,2,192]{2,1,0:T(2,128)(2,1)S(1)}, bf16[2,2,192]{2,1,0:T(2,128)(2,1)}, u32[]{:S(2)}) copy-start(bf16[2,2,192]{2,1,0:T(2,128)(2,1)} %param.11) | copy-start | bytes 4612
  8.8 39.8 %collective-permute-start.4 = (bf16[3,28,384]{2,0,1:T(4,128)(2,1)S(1)}, bf16[3,28,384]{2,0,1:T(4,128)(2,1)S(1)}, u32[]{:S(2)}, u32[]{:S(2)}) collective-permute-start(bf16[3,28,384]{2,0,1:T(4,128)(2,1)S(1)} %copy.277), channel_id=1, source_target_pairs={{0,30},{2,0},{4,2},{6,4},{8,6},{10,8},{12,10},{14,12},{16,14},{18,... | collective-permute-start | bytes 193544 | tf_op jit(solution)/shard_map/ppermute | solution.py:17
  14.3 10.7 %copy-start.69 = (s32[49,49]{1,0:T(8,128)S(1)}, s32[49,49]{1,0:T(8,128)}, u32[]{:S(2)}) copy-start(s32[49,49]{1,0:T(8,128)} %param.18) | copy-start | bytes 28816
  14.3 10.8 %copy-start.82 = (bf16[2,6,169]{2,0,1:T(2,128)(2,1)S(1)}, bf16[2,6,169]{2,0,1:T(2,128)(2,1)}, u32[]{:S(2)}) copy-start(bf16[2,6,169]{2,0,1:T(2,128)(2,1)} %param.16) | copy-start | bytes 12172
  14.3 209.5 %reduce-scatter.25.cloned.1.call-start = ((), (), s32[]{:S(2)}) async-start(), calls=%async_computation.16 | async-start | bytes 442368 | tf_op jit(solution)/shard_map/reduce_scatter | solution.py:266
  14.6 16.5 %copy-start.50 = (f32[4,7,7]{1,2,0:T(8,128)}, f32[4,7,7]{1,2,0:T(8,128)S(1)}, u32[]{:S(2)}) copy-start(f32[4,7,7]{1,2,0:T(8,128)S(1)} %broadcast_multiply_fusion.1) | copy-start | bytes 2356
  14.8 16.3 %copy-start.55 = (f32[4,7,7]{1,2,0:T(8,128)}, f32[4,7,7]{1,2,0:T(8,128)S(1)}, u32[]{:S(2)}) copy-start(f32[4,7,7]{1,2,0:T(8,128)S(1)} %add_rsqrt_fusion.1) | copy-start | bytes 2356
  15.0 15.8 %copy-start.83 = (s32[7,28]{1,0:T(8,128)S(1)}, s32[7,28]{1,0:T(8,128)}, u32[]{:S(2)}) copy-start(s32[7,28]{1,0:T(8,128)} %param.17) | copy-start | bytes 2356
  20.3 11.0 %copy-start.47 = (bf16[2,192,384]{2,1,0:T(8,128)(2,1)S(1)}, bf16[2,192,384]{2,1,0:T(8,128)(2,1)}, u32[]{:S(2)}) copy-start(bf16[2,192,384]{2,1,0:T(8,128)(2,1)} %param.13) | copy-start | bytes 884740
  25.0 21.1 %copy-start.61 = (f32[384]{0:T(512)}, f32[384]{0:T(512)S(1)}, u32[]{:S(2)}) copy-start(f32[384]{0:T(512)S(1)} %get-tuple-element.55) | copy-start | bytes 4612
  25.0 112.0 %copy-start.63 = (f32[384]{0:T(512)}, f32[384]{0:T(512)S(1)}, u32[]{:S(2)}) copy-start(f32[384]{0:T(512)S(1)} %get-tuple-element.53) | copy-start | bytes 4612
  25.1 5.8 %copy-start.78 = (s32[2401]{0:T(1024)}, s32[2401]{0:T(1024)S(1)}, u32[]{:S(2)}) copy-start(s32[2401]{0:T(1024)S(1)} %eq.20) | copy-start | bytes 28816
  46.1 12.2 %copy-start = (bf16[2,384,384]{2,1,0:T(8,128)(2,1)}, bf16[2,384,384]{2,1,0:T(8,128)(2,1)S(1)}, u32[]{:S(2)}) copy-start(bf16[2,384,384]{2,1,0:T(8,128)(2,1)S(1)} %all_gather.21) | copy-start | bytes 1769476
  47.4 10.9 %copy-start.3 = (f32[196,384]{1,0:T(8,128)}, f32[196,384]{1,0:T(8,128)S(1)}, u32[]{:S(2)}) copy-start(f32[196,384]{1,0:T(8,128)S(1)} %reshape.346) | copy-start | bytes 903172
  49.2 80.7 %collective-permute-start.5 = (bf16[7,3,384]{2,0,1:T(8,128)(2,1)}, bf16[7,3,384]{2,0,1:T(8,128)(2,1)}, u32[]{:S(2)}, u32[]{:S(2)}) collective-permute-start(bf16[7,3,384]{2,0,1:T(8,128)(2,1)} %pad_maximum_fusion.8), channel_id=1, source_target_pairs={{0,1},{1,0},{2,3},{3,2},{4,5},{5,4},{6,7},{7,6},{8,9},{9,8},{10,11... | collective-permute-start | bytes 48392 | tf_op jit(solution)/shard_map/ppermute | solution.py:17
  52.9 3.1 copy-start.8
  53.3 2.7 copy-start.10
  57.7 28.3 %copy-start.65 = (f32[384]{0:T(512)S(1)}, f32[384]{0:T(512)}, u32[]{:S(2)}) copy-start(f32[384]{0:T(512)} %get-tuple-element.54) | copy-start | bytes 4612
  58.3 30.5 %copy-start.18 = (bf16[196,384]{0,1:T(8,128)(2,1)}, bf16[196,384]{0,1:T(8,128)(2,1)S(1)}, u32[]{:S(2)}) copy-start(bf16[196,384]{0,1:T(8,128)(2,1)S(1)} %convert_element_type.284) | copy-start | bytes 451588
  58.7 30.1 %copy-start.70 = (f32[196]{0:T(256)}, f32[196]{0:T(256)S(1)}, u32[]{:S(2)}) copy-start(f32[196]{0:T(256)S(1)} %broadcast_multiply_fusion.11) | copy-start | bytes 2356
  58.9 29.9 %copy-start.74 = (f32[196]{0:T(256)}, f32[196]{0:T(256)S(1)}, u32[]{:S(2)}) copy-start(f32[196]{0:T(256)S(1)} %add_rsqrt_fusion.3) | copy-start | bytes 2356
  126.0 6.0 %collective-permute-start = (bf16[3,28,384]{2,0,1:T(4,128)(2,1)S(1)}, bf16[3,28,384]{2,0,1:T(4,128)(2,1)S(1)}, u32[]{:S(2)}, u32[]{:S(2)}) collective-permute-start(bf16[3,28,384]{2,0,1:T(4,128)(2,1)S(1)} %bitcast.249), channel_id=1, source_target_pairs={{0,30},{2,0},{4,2},{6,4},{8,6},{10,8},{12,10},{14,12},{16,14},{18,... | collective-permute-start | bytes 193544 | tf_op jit(solution)/shard_map/ppermute | solution.py:17
  130.8 28.5 %copy-start.41 = (bf16[196,384]{1,0:T(8,128)(2,1)}, bf16[196,384]{1,0:T(8,128)(2,1)S(1)}, u32[]{:S(2)}) copy-start(bf16[196,384]{1,0:T(8,128)(2,1)S(1)} %reshape.354) | copy-start | bytes 451588
  132.0 3.8 collective-permute-start.1
  153.8 5.6 %copy-start.72 = (f32[196]{0:T(256)}, f32[196]{0:T(256)S(1)}, u32[]{:S(2)}) copy-start(f32[196]{0:T(256)S(1)} %broadcast_multiply_fusion.10) | copy-start | bytes 2356
  154.0 5.4 copy-start.76
  172.7 3.3 copy-start.36
  172.7 3.4 copy-start.5
  172.7 3.4 copy-start.64
  176.1 2.7 copy-start.31
  179.1 3.8 collective-permute-start.6
  180.7 44.7 %reduce-scatter.23.cloned.1.call-start = ((), (), s32[]{:S(2)}) async-start(), calls=%async_computation.15 | async-start | bytes 442368 | tf_op jit(solution)/shard_map/reduce_scatter | solution.py:248
  183.0 6.7 %collective-permute-start.7 = (bf16[3,28,384]{2,0,1:T(4,128)(2,1)S(1)}, bf16[3,28,384]{2,0,1:T(4,128)(2,1)S(1)}, u32[]{:S(2)}, u32[]{:S(2)}) collective-permute-start(bf16[3,28,384]{2,0,1:T(4,128)(2,1)S(1)} %fusion.94), channel_id=1, source_target_pairs={{0,2},{2,4},{4,6},{6,8},{8,10},{10,12},{12,14},{14,16},{16,18},{18... | collective-permute-start | bytes 193544 | tf_op jit(solution)/shard_map/ppermute | solution.py:17
  189.8 4.3 copy-start.42
  189.9 3.0 copy-start.16
  189.9 3.0 copy-start.66
  189.9 3.0 copy-start.71
  189.9 3.0 copy-start.75
  195.3 32.2 %reduce-scatter.21.cloned.1.call-start = ((), (), s32[]{:S(2)}) async-start(), calls=%async_computation.14 | async-start | bytes 1327104 | tf_op jit(solution)/shard_map/reduce_scatter | solution.py:263
  196.4 7.0 %copy-start.44 = (f32[4,12,49]{2,1,0:T(8,128)}, f32[4,12,49]{2,1,0:T(8,128)S(1)}, u32[]{:S(2)}) copy-start(f32[4,12,49]{2,1,0:T(8,128)S(1)} %log_add_fusion) | copy-start | bytes 28228
  196.4 2.8 copy-start.2
  199.1 49.2 %reduce-scatter.19.cloned.1.call-start = ((), (), s32[]{:S(2)}) async-start(), calls=%async_computation.13 | async-start | bytes 1327104 | tf_op jit(solution)/shard_map/reduce_scatter | solution.py:245
  200.4 3.0 copy-start.22
  209.4 63.6 %reduce-scatter.29.cloned.1.call-start = ((), (), s32[]{:S(2)}) async-start(), calls=%async_computation.18 | async-start | bytes 1769472 | tf_op jit(solution)/shard_map/reduce_scatter | solution.py:269
  211.2 85.9 %reduce-scatter.33.cloned.1.call-start = ((), (), s32[]{:S(2)}) async-start(), calls=%async_computation.20 | async-start | bytes 1769472 | tf_op jit(solution)/shard_map/reduce_scatter | solution.py:272
  213.9 2.8 copy-start.43
  213.9 107.1 %reduce-scatter.27.cloned.1.call-start = ((), (), s32[]{:S(2)}) async-start(), calls=%async_computation.17 | async-start | bytes 1769472 | tf_op jit(solution)/shard_map/reduce_scatter | solution.py:251
  216.6 3.3 copy-start.86
  216.6 3.3 copy-start.85
  216.6 128.5 %reduce-scatter.31.cloned.1.call-start = ((), (), s32[]{:S(2)}) async-start(), calls=%async_computation.19 | async-start | bytes 1769472 | tf_op jit(solution)/shard_map/reduce_scatter | solution.py:254
  216.7 4.1 copy-start.17
  219.8 138.1 %reduce-scatter.37.cloned.1.call-start = ((), (), s32[]{:S(2)}) async-start(), calls=%async_computation.22 | async-start | bytes 147456
  220.8 150.2 %reduce-scatter.35.cloned.1.call-start = ((), (), s32[]{:S(2)}) async-start(), calls=%async_computation.21 | async-start | bytes 147456
  223.5 305.5 %all-reduce.9.cloned.1.call-start = ((), (), s32[]{:S(2)}) async-start(), calls=%async_computation.23 | async-start | bytes 14155776 | tf_op jit(solution)/shard_map/psum | solution.py:279
  352.4 6.4 %collective-permute-start.2 = (bf16[7,3,384]{2,0,1:T(8,128)(2,1)S(1)}, bf16[7,3,384]{2,0,1:T(8,128)(2,1)S(1)}, u32[]{:S(2)}, u32[]{:S(2)}) collective-permute-start(bf16[7,3,384]{2,0,1:T(8,128)(2,1)S(1)} %slice.194), channel_id=1, source_target_pairs={{0,1},{1,0},{2,3},{3,2},{4,5},{5,4},{6,7},{7,6},{8,9},{9,8},{10,11... | collective-permute-start | bytes 48392 | tf_op jit(solution)/shard_map/ppermute | solution.py:17
  358.9 10.2 %collective-permute-start.3 = (bf16[3,28,384]{2,0,1:T(4,128)(2,1)S(1)}, bf16[3,28,384]{2,0,1:T(4,128)(2,1)S(1)}, u32[]{:S(2)}, u32[]{:S(2)}) collective-permute-start(bf16[3,28,384]{2,0,1:T(4,128)(2,1)S(1)} %fusion.95), channel_id=1, source_target_pairs={{0,2},{2,4},{4,6},{6,8},{8,10},{10,12},{12,14},{14,16},{16,18},{18... | collective-permute-start | bytes 193544 | tf_op jit(solution)/shard_map/ppermute | solution.py:17
  365.4 5.2 collective-permute-start.8
  367.6 3.2 collective-permute-start.9
  528.9 3.3 copy-start.29
  528.9 3.3 copy-start.30
  (52 other events, 77.4 us)
Sparse Core Ops, SparseCore 0:
  9.6 38.7 all-gather.3
  49.9 36.0 all-gather.5
  87.6 36.0 all-gather.7
  180.8 11.8 reduce-scatter.24
  195.4 11.3 reduce-scatter.22
  209.0 18.5 reduce-scatter.20
  229.8 18.5 reduce-scatter.18
  251.2 21.7 reduce-scatter.28
  275.3 21.7 reduce-scatter.32
  299.2 21.7 reduce-scatter.26
  323.3 21.7 reduce-scatter.30
  347.7 10.1 reduce-scatter.36
  360.1 9.9 reduce-scatter.34
  375.2 153.7 all-reduce.8
where the time goes:
time: 554 us; the launch traced here: 544 us
  waiting for transfers between devices  280 us (51%)
  blocking collectives  93.2 us (17%)
  matrix products  53.5 us (10%)
  local copies, waits for them, and re-layouts  46.1 us (8%)
  other arithmetic  36.7 us (7%)
  starting transfers between devices  17.1 us (3%)
  between operations  16.8 us (3%)
    psum x1, waiting for transfers between devices, per_device(): lax.psum((shards[0], shards[1], shards[2], shards[3], shards[4], shards[5...  92.4 us
    psum x1, blocking collectives, per_device(): lax.psum((shards[0], shards[1], shards[2], shards[3], shards[4], shards[5...  63.5 us
    all_gather x1, waiting for transfers between devices, per_device(): lax.all_gather(w_down, 'fsdp', axis=1, tiled=True)  34.8 us
    all_gather x1, waiting for transfers between devices, per_device(): lax.all_gather(w_up, 'fsdp', axis=1, tiled=True)  27.1 us
    another operation x18, other arithmetic, per_device(): jnp.stack([summed[index], summed[index + 6]])  23.8 us
    reduce_scatter x1, waiting for transfers between devices, per_device(): lax.psum_scatter(grads_two[3].astype(jnp.bfloat16), 'fsdp', scatter_dimen...  22.6 us
    reduce_scatter x1, waiting for transfers between devices, per_device(): lax.psum_scatter(grads_two[4].astype(jnp.bfloat16), 'fsdp', scatter_dimen...  21.9 us
    reduce_scatter x1, waiting for transfers between devices, per_device(): lax.psum_scatter(grads_one[4].astype(jnp.bfloat16), 'fsdp', scatter_dimen...  21.9 us
  transfers between devices with their start and end apart: 24, of which 14 were waited for; matrix products, arithmetic and copies ran while one was open for 16% of the time, Pallas kernels for 0%

commit v1 on v0

v1 whole, which is shorter than its diff:
```python
import functools
import types

import jax
import jax.numpy as jnp
from jax import lax
from jax.experimental import pallas as pl
from jax.experimental.pallas import tpu as pltpu
from jax.sharding import PartitionSpec as P

WIN = 7
SHIFT = 3
TABLE = 169
SIDE = 8
SLOT = SIDE * SIDE
HEAD = 32
PAIR = 2 * SLOT
EPSILON = 1e-05
MASKED_SCORE = -1000000000.0
F32 = jnp.float32
BF16 = jnp.bfloat16
VMEM_LIMIT = 24 * 1024 * 1024
PACK_VMEM_LIMIT = 60 * 1024 * 1024
BYTES_PER_US = 3500000


def exchange(array, ds, dy):
    n, m = lax.axis_size("seq"), lax.axis_size("fsdp")
    pairs = [(s * m + y, (s ^ ds) * m + (y ^ dy)) for s in range(n) for y in range(m)]
    return lax.ppermute(array, ("seq", "fsdp"), pairs)


def take_from(array, ds, dy):
    n, m = lax.axis_size("seq"), lax.axis_size("fsdp")
    pairs = [((s + ds) % n * m + (y + dy) % m, s * m + y) for s in range(n) for y in range(m)]
    return lax.ppermute(array, ("seq", "fsdp"), pairs)


def halo(near_rows, near_cols, corner, step):
    return (
        take_from(near_rows, step, 0),
        take_from(near_cols, 0, step),
        take_from(corner, step, step),
    )


def share_halves(piece, after=()):
    first = exchange(piece, 0, 1)
    if after:
        first = tie(first, after)
    return (first, exchange(first, 1, 0))


def add(*terms):
    total = terms[0].astype(F32)
    for term in terms[1:]:
        total = total + term.astype(F32)
    return total


def sum_higher(value):
    step = 16
    while step < lax.axis_size("seq"):
        value = add(value, exchange(value, step, 0)).astype(value.dtype)
        step *= 2
    return value


def start_cube(keep, got, small):
    kinds, _, rows, cols = keep.shape[2:]
    count = small[0].shape[0]
    out = shape_of(kinds * 2 * rows + count, cols)
    ins = {"keep": (VMEM, keep), "got": (VMEM, got)} | numbered("small", VMEM, small)
    r = call(add_core_kernel, "add_core", ins, {"out" + str(i): out for i in range(8)}, {})
    outs = listed(r, "out")
    return [outs[0]] + [
        exchange(outs[i], (i >> 1 & 1) * 2 + (i & 1) * 4, i >> 2) for i in (7, 6, 5, 4, 3, 2, 1)
    ]


def start_side(keeps, gots, after=()):
    kinds = sum(keep.shape[2] for keep in keeps)
    out = shape_of(2, kinds, *keeps[0].shape[3:])
    ins = numbered("keep", VMEM, keeps) | numbered("got", VMEM, gots)
    r = call(add_side_kernel, "add_side", ins, {"own": out, "other": out}, {}, after)
    return r.own, exchange(r.other, 0, 1)


def start_face(parts, after=()):
    _, kinds, _, rows, cols = parts[0].shape
    out = shape_of(kinds * 2 * rows, cols)
    ins = numbered("part", VMEM, parts)
    outs = {"out" + str(i): out for i in range(4)}
    r = call(add_face_kernel, "add_face", ins, outs, {}, after)
    return r.out0, exchange(r.out3, 6, 0), exchange(r.out2, 2, 0), exchange(r.out1, 4, 0)


def finish_sum(parts, rows, after=()):
    kinds = parts[0].shape[0] // (2 * rows)
    out = shape_of(parts[0].shape[0] - kinds * rows, parts[0].shape[1])
    kernel = functools.partial(halve_kernel, kinds, rows)
    ins = numbered("part", VMEM, parts)
    r = call(kernel, "halve", ins, {"own": out, "other": out}, {}, after)
    return sum_higher(add(r.own, exchange(r.other, 8, 0)).astype(BF16))


def gather(total, rows, after=()):
    ins = {"own": (VMEM, total), "other": (VMEM, exchange(total, 8, 0))}
    out = shape_of(2, rows, total.shape[1])
    pair = call(stack_kernel, "stack", ins, {"out": out}, {}, after).out
    here = [pair, exchange(pair, 4, 0), exchange(pair, 2, 0), exchange(pair, 6, 0)]
    return here + [exchange(part, 1, 0) for part in here]


def flip(index, bits):
    return jnp.bitwise_xor(index, bits)


def pack_kernel(layer, r):
    core = r.place[0]
    width_c = r.proj.shape[2]
    rows = r.qkv.shape[1] // 2
    if layer == 0:
        attend, mlp = r.attend, r.mlp
    else:
        attend, mlp = r.both.at[:rows], r.both.at[rows:]
    start = pl.multiple_of(core * rows, 16)
    pairs = [
        (r.qkv.at[layer, pl.ds(start, rows), :], attend.at[:, : 3 * width_c]),
        (r.proj.at[layer, pl.ds(start, rows), :], attend.at[:, 3 * width_c :]),
        (r.up.at[layer, pl.ds(start, rows), :], mlp.at[:rows]),
    ]
    for index in range(4):
        first = pl.multiple_of((core * 4 + index) * rows, 16)
        cols = slice(index * width_c, (index + 1) * width_c)
        pairs.append((r.down.at[layer, pl.ds(first, rows), :], mlp.at[rows:, cols]))
    copies = start_copies(pairs, r.sems)
    wait_all(copies)


def pack_small_kernel(r):
    r.small[...] = jnp.zeros_like(r.small)
    for index in range(2):
        r.small[2 * index : 2 * index + 2, : r.gains.shape[2]] = r.gains[index].astype(F32)
        first = 4 + index * r.tables.shape[1]
        r.small[first : first + r.tables.shape[1], :TABLE] = r.tables[index].astype(F32)


def table_sums_kernel(r):
    heads = r.grad0.shape[0]
    total = jnp.zeros((2 * heads, TABLE), F32)
    for key in range(SLOT):
        pair = jnp.concatenate([r.grad0[:, key, :], r.grad1[:, key, :]], axis=0)
        total = total + mm(pair.astype(BF16), r.onehot[key])
    r.wide[...] = jnp.zeros_like(r.wide)
    half = r.out.shape[1] // 2
    r.wide[:heads, :TABLE] = total[:heads]
    r.wide[:heads, half : half + TABLE] = total[heads:]
    r.out[...] = r.wide[...].astype(BF16)


def params_kernel(r):
    half = r.gains.shape[2] // 2
    heads = r.table.shape[1] // 2
    flipped = r.place[3] == 1
    first = jnp.where(flipped, r.other[...], r.own[...])
    second = jnp.where(flipped, r.own[...], r.other[...])
    for index in range(2):
        for part, value in ((0, first), (1, second)):
            r.gains[index, :, part * half : (part + 1) * half] = value[
                2 * index : 2 * index + 2, :half
            ]
            rows = value[4 + index * heads : 4 + (index + 1) * heads, :TABLE]
            r.table[index, part * heads : (part + 1) * heads, :] = rows


def start_copies(pairs, sems):
    copies = [
        pltpu.make_async_copy(source, target, sems.at[index])
        for index, (source, target) in enumerate(pairs)
    ]
    for copy in copies:
        copy.start()
    return copies


def fetch(place, layer, own, parts, pick, full, sems):
    half = full.shape[0] // 2
    rows = half // len(parts)
    y = place[3]
    pairs = [(own.at[layer], full.at[pl.ds(pl.multiple_of(y * half, 16), half)])]
    for spot, part in zip((place[0], flip(place[0], 1)), parts):
        pieces = pick(part)
        count = rows // len(pieces)
        for index, piece in enumerate(pieces):
            start = pl.multiple_of((1 - y) * half + spot * rows + index * count, 16)
            pairs.append((piece, full.at[pl.ds(start, count)]))
    return start_copies(pairs, sems)


def fetch_attend(place, layer, own, parts, qkv_w, proj_w, sems):
    rows = own[0].shape[1] // 2
    wide = qkv_w.shape[1]

    def qkv(part):
        return [part.at[:rows, :wide]]

    def proj(part):
        return [part.at[:rows, wide:]]

    return (
        fetch(place, layer, own[0], parts, qkv, qkv_w, sems.at[0]),
        fetch(place, layer, own[1], parts, proj, proj_w, sems.at[1]),
    )


def fetch_mlp(place, layer, own, parts, up_w, down_w, sems):
    rows = own[0].shape[1] // 2
    first = parts[0].shape[0] - 2 * rows
    width_c = down_w.shape[1]

    def up(part):
        return [part.at[first : first + rows]]

    def down(part):
        return [part.at[first + rows :, i * width_c : (i + 1) * width_c] for i in range(4)]

    return (
        fetch(place, layer, own[0], parts, up, up_w, sems.at[0]),
        fetch(place, layer, own[1], parts, down, down_w, sems.at[1]),
    )


def add_refs(refs):
    total = refs[0][...].astype(F32)
    for ref in refs[1:]:
        total = total + ref[...].astype(F32)
    return total


def add_core_kernel(r):
    kinds, _, rows, _ = r.keep.shape[2:]
    small = (r.small0[...].astype(F32) + r.small1[...].astype(F32)).astype(BF16)
    for index, out in enumerate(listed(r, "out")):
        y, x, z = index >> 2, index >> 1 & 1, index & 1
        for kind in range(kinds):
            for high in range(2):
                at = (y, x, kind, 2 * high + z)
                first = (kind * 2 + high) * rows
                value = r.keep[at].astype(F32) + r.got[at].astype(F32)
                out[first : first + rows, :] = value.astype(BF16)
        out[kinds * 2 * rows :, :] = small


def add_side_kernel(r):
    for y, out in enumerate((r.own, r.other)):
        first = 0
        for keep, got in zip(listed(r, "keep"), listed(r, "got")):
            for x in range(2):
                value = keep[y, x].astype(F32) + got[y, x].astype(F32)
                out[x, first : first + keep.shape[2]] = value.astype(BF16)
            first += keep.shape[2]


def add_face_kernel(r):
    _, kinds, _, rows, _ = r.part0.shape
    for index, out in enumerate(listed(r, "out")):
        x, z = index >> 1, index & 1
        for kind in range(kinds):
            for high in range(2):
                at = (x, kind, 2 * high + z)
                first = (kind * 2 + high) * rows
                value = r.part0[at].astype(F32) + r.part1[at].astype(F32)
                out[first : first + rows, :] = value.astype(BF16)


def halve_kernel(kinds, rows, r):
    parts = listed(r, "part")
    for high, out in enumerate((r.own, r.other)):
        for kind in range(kinds):
            first = (kind * 2 + high) * rows
            value = add_refs([part.at[first : first + rows, :] for part in parts])
            out[kind * rows : (kind + 1) * rows, :] = value.astype(BF16)
        if out.shape[0] > kinds * rows:
            value = add_refs([part.at[kinds * 2 * rows :, :] for part in parts])
            out[kinds * rows :, :] = value.astype(BF16)


def stack_kernel(r):
    rows = r.out.shape[1]
    r.out[0] = r.own[:rows, :]
    r.out[1] = r.other[:rows, :]


def wait_all(copies):
    for copy in copies:
        copy.wait()


def row_segments(mode, refs, row, width):
    if mode == "plain":
        return [(0, refs[0][row], 0, width)]
    own, rows, cols, corner = refs
    rest = width - SHIFT
    if mode == "in":
        if row < WIN - SHIFT:
            return [
                (0, own[row + SHIFT], SHIFT, rest),
                (rest, cols[row + SHIFT], 0, SHIFT),
            ]
        at = row - (WIN - SHIFT)
        return [(0, rows[at], SHIFT, rest), (rest, corner[at], 0, SHIFT)]
    if row >= SHIFT:
        return [(0, cols[row - SHIFT], 0, SHIFT), (SHIFT, own[row - SHIFT], 0, rest)]
    return [(0, corner[row], 0, SHIFT), (SHIFT, rows[row], 0, rest)]


def fill_windows(mode, refs, out):
    width = refs[0].shape[1]
    out[...] = jnp.zeros_like(out)
    for row in range(WIN):
        for first, source, start, count in row_segments(mode, refs, row, width):
            source = source.astype(F32)
            for window in range(width // WIN):
                low = max(first, window * WIN)
                high = min(first + count, window * WIN + WIN)
                if low < high:
                    spot = window * SLOT + row * SIDE + low - window * WIN
                    begin = start + low - first
                    out[spot : spot + high - low, :] = source[begin : begin + high - low, :]


def fill_grid(source, buffer, width):
    for row in range(WIN):
        for window in range(width // WIN):
            spot = window * SLOT + row * SIDE
            buffer[row, window * WIN : window * WIN + WIN, :] = source[spot : spot + WIN, :]


def normalize(values):
    centred = values - jnp.mean(values, -1, keepdims=True)
    factor = lax.rsqrt(jnp.mean(centred * centred, -1, keepdims=True) + EPSILON)
    return centred * factor, factor


def normalize_back(grad_norm, normed, factor):
    spread = jnp.mean(grad_norm * normed, -1, keepdims=True)
    return factor * (grad_norm - jnp.mean(grad_norm, -1, keepdims=True) - normed * spread)


def mm(left, right):
    return lax.dot_general(left, right, (((1,), (0,)), ((), ())), preferred_element_type=F32)


def mm_nt(left, right):
    return lax.dot_general(left, right, (((1,), (1,)), ((), ())), preferred_element_type=F32)


def only_head(group, which):
    rows = lax.broadcasted_iota(jnp.int32, group.shape, 0)
    inside = (rows >= which * HEAD) & (rows < (which + 1) * HEAD)
    return jnp.where(inside, group, jnp.zeros_like(group))


def diagonal(block):
    lanes = lax.broadcasted_iota(jnp.int32, (SLOT, PAIR), 1)
    return jnp.where(lanes < SLOT, block[:SLOT], block[SLOT:])


def spread_diagonal(packed):
    lanes = lax.broadcasted_iota(jnp.int32, (SLOT, PAIR), 1)
    low = jnp.where(lanes < SLOT, packed, 0.0)
    high = jnp.where(lanes < SLOT, 0.0, packed)
    return jnp.concatenate([low, high], axis=0).astype(BF16)


def store_columns(r, out, x, kind, value):
    rows = value.shape[0] // 8
    value = value.astype(BF16)
    for y in range(2):
        for z in range(4):
            first = (y * 4 + z) * rows
            at = (flip(r.place[3], y), flip(r.place[1], x), kind, flip(r.place[2], z))
            out[at] = value[first : first + rows]


def store_rows(r, out, y, kind, value):
    rows = value.shape[0] // 8
    value = value.astype(BF16)
    for x in range(2):
        for z in range(4):
            first = (x * 4 + z) * rows
            at = (flip(r.place[3], y), flip(r.place[1], x), kind, flip(r.place[2], z))
            out[at] = value[first : first + rows]


def grid_refs(r, which):
    if not hasattr(r, "rows_in"):
        return [r.own]
    return [r.own if which == 0 else r.own_two] + [
        edge.at[which] for edge in (r.rows_in, r.cols_in, r.corner_in)
    ]


def attend_forward_kernel(layer, mode, r):
    width_c = r.flat.shape[1]
    heads = width_c // HEAD
    copies = fetch_attend(
        r.place, layer, (r.qkv, r.proj), listed(r, "a_part"), r.qkv_w, r.proj_w, r.a_sems
    )
    fill_windows(mode, grid_refs(r, 0), r.flat)
    r.x[...] = r.flat[...].astype(BF16)
    normed, _ = normalize(r.flat[...])
    hidden = (normed * r.gains[layer, 0:1, :]).astype(BF16)
    wait_all(copies[0])
    query = (mm(hidden, r.qkv_w[:, :width_c]) * HEAD ** (-0.5)).astype(BF16)
    r.query_t[...] = query.T
    r.keys[...] = mm(hidden, r.qkv_w[:, width_c : 2 * width_c]).astype(BF16)
    r.keys_t[...] = r.keys[...].T
    r.values[...] = mm(hidden, r.qkv_w[:, 2 * width_c :]).astype(BF16)
    r.values_t[...] = r.values[...].T
    if mode == "plain":
        place = lax.broadcasted_iota(jnp.int32, (SLOT, PAIR), 0)
        meet = (place < WIN * SIDE) & (jnp.bitwise_and(place, SIDE - 1) < WIN)
    for head in range(heads):
        group = slice(head // 4 * 128, head // 4 * 128 + 128)
        rows = slice(head * HEAD, head * HEAD + HEAD)
        for pair in range(r.flat.shape[0] // PAIR):
            span = slice(pair * PAIR, pair * PAIR + PAIR)
            raw = mm(r.keys[span, group], only_head(r.query_t[group, span], head % 4))
            if mode != "plain":
                meet = r.same[:, span] > 0.5
            scores = jnp.where(meet, diagonal(raw) + r.bias[layer, head], MASKED_SCORE)
            weighted = jnp.exp(scores - jnp.max(scores, 0, keepdims=True))
            attention = weighted / jnp.sum(weighted, 0, keepdims=True)
            r.probs[head, :, span] = attention
            r.mixed_t[rows, span] = mm(r.values_t[rows, span], spread_diagonal(attention)).astype(
                BF16
            )
    wait_all(copies[1])
    r.middle[...] = r.flat[...] + mm(r.mixed_t[...].T, r.proj_w[...])


def attend_backward_kernel(layer, parts, kind, r):
    width_c = r.x.shape[1]
    heads = width_c // HEAD
    if "s" in parts or "i" in parts:
        copies = fetch_attend(
            r.place, layer, (r.qkv, r.proj), listed(r, "a_part"), r.qkv_w, r.proj_w, r.a_sems
        )
    normed, factor = normalize(r.x[...].astype(F32))
    gain = r.gains[layer, 0:1, :]
    attended = r.grad_m[...].astype(BF16)
    if "s" in parts:
        wait_all(copies[1])
        r.out_t[...] = mm_nt(r.proj_w[...], attended).astype(BF16)
        for head in range(heads):
            group = slice(head // 4 * 128, head // 4 * 128 + 128)
            rows = slice(head * HEAD, head * HEAD + HEAD)
            row_k = slice(width_c + head * HEAD, width_c + head * HEAD + HEAD)
            row_v = slice(2 * width_c + head * HEAD, 2 * width_c + head * HEAD + HEAD)
            total = jnp.zeros((SLOT, PAIR), F32)
            for pair in range(r.x.shape[0] // PAIR):
                span = slice(pair * PAIR, pair * PAIR + PAIR)
                attention = r.probs[head, :, span]
                grad_p = diagonal(
                    mm(r.values[span, group], only_head(r.out_t[group, span], head % 4))
                )
                grad_s = attention * (grad_p - jnp.sum(grad_p * attention, 0, keepdims=True))
                total = total + grad_s
                spread_p = spread_diagonal(attention)
                spread_s = spread_diagonal(grad_s)
                grad_q = mm(r.keys_t[rows, span], spread_s) * HEAD ** (-0.5)
                r.grad_t[rows, span] = grad_q.astype(BF16)
                r.grad_t[row_k, span] = mm_nt(r.query_t[rows, span], spread_s).astype(BF16)
                r.grad_t[row_v, span] = mm_nt(r.out_t[rows, span], spread_p).astype(BF16)
            r.bias_grad[head] = total
    if "w" in parts:
        r.left[0] = (normed * gain).astype(BF16).T
        r.left[1] = r.mixed_t[...]
        r.right[: 3 * width_c, :] = r.grad_t[...]
        r.right[3 * width_c :, :] = attended.T
        for apart, out in ((1, r.send), (0, r.keep)):
            for x in range(2):
                chunk = 2 * flip(r.place[0], apart) + x
                left = r.left[(chunk == 3).astype(jnp.int32)]
                right = r.right[pl.ds(pl.multiple_of(chunk * width_c, 128), width_c), :]
                store_columns(r, out, x, kind, mm_nt(left, right))
    if "s" in parts or "i" in parts:
        if "s" not in parts:
            wait_all(copies[1])
        wait_all(copies[0])
    if "i" in parts:
        grad_hidden = mm(r.qkv_w[...], r.grad_t[...]).T
        r.flat[...] = r.grad_m[...] + normalize_back(grad_hidden * gain, normed, factor)
        width = r.grid.shape[1]
        fill_grid(r.flat, r.buffer, width)
        r.grid[...] = r.buffer[:, :width, :].astype(BF16)
        if hasattr(r, "rows"):
            r.rows[0] = r.buffer[WIN - SHIFT :, :width, :].astype(BF16)
            r.cols[0] = r.buffer[:, width - SHIFT : width, :].astype(BF16)
            r.corner[0] = r.buffer[WIN - SHIFT :, width - SHIFT : width, :].astype(BF16)


GELU_A = 0.7978845608028654
GELU_B = 0.044715


def gelu_parts(inner):
    square = inner * inner
    tanh = jnp.tanh(GELU_A * (inner * (1.0 + GELU_B * square)))
    return square, tanh


def mlp_forward_kernel(layer, r):
    width_c = r.flat.shape[1]
    copies = fetch_mlp(
        r.place, layer, (r.up, r.down), listed(r, "m_part"), r.up_w, r.down_w, r.m_sems
    )
    normed, _ = normalize(r.middle[...])
    hidden = (normed * r.gains[layer, 1:2, :]).astype(BF16)
    output = r.middle[...]
    wait_all(copies[0])
    wait_all(copies[1])
    for chunk in range(r.up_w.shape[1] // width_c):
        cols = slice(chunk * width_c, (chunk + 1) * width_c)
        inner = mm(hidden, r.up_w[:, cols])
        _, tanh = gelu_parts(inner)
        output = output + mm((0.5 * inner * (1.0 + tanh)).astype(BF16), r.down_w[cols, :])
    r.flat[...] = output
    width = r.grid.shape[1]
    fill_grid(r.flat, r.buffer, width)
    r.grid[...] = r.buffer[:, :width, :].astype(BF16)
    r.rows[0] = r.buffer[:SHIFT, :width, :].astype(BF16)
    r.cols[0] = r.buffer[:, :SHIFT, :].astype(BF16)
    r.corner[0] = r.buffer[:SHIFT, :SHIFT, :].astype(BF16)
    r.rows[1] = r.top[:SHIFT]
    r.cols[1] = r.top[:, :SHIFT, :]
    r.corner[1] = r.top[:SHIFT, :SHIFT, :]


def mlp_backward_kernel(layer, mode, which, r):
    width_c = r.flat.shape[1]
    copies = fetch_mlp(
        r.place, layer, (r.up, r.down), listed(r, "m_part"), r.up_w, r.down_w, r.m_sems
    )
    normed, factor = normalize(r.middle[...])
    gain = r.gains[layer, 1:2, :]
    hidden = (normed * gain).astype(BF16)
    hidden_t = hidden.T
    fill_windows(mode, grid_refs(r, which), r.flat)
    grad_low = r.flat[...].astype(BF16)
    forward = hasattr(r, "out")
    output = r.middle[...]
    grad_hidden = jnp.zeros(r.flat.shape, F32)
    wait_all(copies[0])
    wait_all(copies[1])
    outs = (r.keep, r.send)
    for up_apart, down_apart in ((1, 1), (1, 0), (0, 1), (0, 0)):
        high, low = flip(r.place[0], up_apart), flip(r.place[0], down_apart)
        cols = pl.ds(pl.multiple_of((2 * high + low) * width_c, 128), width_c)
        inner = mm(hidden, r.up_w[:, cols])
        square, tanh = gelu_parts(inner)
        activated = (0.5 * inner * (1.0 + tanh)).astype(BF16)
        slope = 0.5 * (1.0 + tanh) + (0.5 * GELU_A) * inner * (1.0 - tanh * tanh) * (
            1.0 + 3.0 * GELU_B * square
        )
        if forward:
            output = output + mm(activated, r.down_w[cols, :])
        store_rows(r, outs[down_apart], high, 1, mm(activated.T, grad_low))
        grad_inner = (mm_nt(grad_low, r.down_w[cols, :]) * slope).astype(BF16)
        store_columns(r, outs[up_apart], low, 0, mm(hidden_t, grad_inner))
        grad_hidden = grad_hidden + mm_nt(grad_inner, r.up_w[:, cols])
    r.grad_m[...] = r.flat[...] + normalize_back(grad_hidden * gain, normed, factor)
    if forward:
        r.flat[...] = output
        width = r.out.shape[1]
        fill_grid(r.flat, r.buffer, width)
        r.out[...] = r.buffer[:, :width, :].astype(BF16)
        r.rows[1] = r.buffer[WIN - SHIFT :, :width, :].astype(BF16)
        r.cols[1] = r.buffer[:, width - SHIFT : width, :].astype(BF16)
        r.corner[1] = r.buffer[WIN - SHIFT :, width - SHIFT : width, :].astype(BF16)


def roll_out_kernel(r):
    refs = grid_refs(r, 1)
    width = r.mixed.shape[1]
    for row in range(WIN):
        for first, source, start, count in row_segments("out", refs, row, width):
            r.buffer[row, first : first + count, :] = source.astype(F32)[start : start + count, :]
    r.mixed[...] = r.buffer[:, :width, :].astype(BF16)


def collect_kernel(layer, r):
    rows, cols = r.table.shape[-2:]
    half = r.qkv.shape[1]
    for index, ref in enumerate(listed(r, "all")):
        for high in range(2):
            for kind in range(3):
                piece = ref[high, kind * rows : (kind + 1) * rows, :]
                r.table[index >> 2, index >> 1 & 1, 2 * high + (index & 1), kind] = piece
    for core in range(2):
        for x in range(2):
            chunk = 2 * core + x
            for z in range(4):
                at = (flip(r.place[0], core), flip(r.place[1], x), flip(r.place[2], z))
                band = slice(z * rows, (z + 1) * rows)
                span = slice(chunk * cols, (chunk + 1) * cols)
                r.up[0, band, span] = r.table[at + (0,)].astype(F32)
                first = (chunk * 4 + z) * rows
                r.down[0, first : first + rows, :] = r.table[at + (1,)].astype(F32)
                piece = r.table[at + (2,)].astype(F32)
                if chunk < 3:
                    r.qkv[0, band, span] = piece
                else:
                    r.proj[0, band, :] = piece
    r.wide[...] = jnp.zeros_like(r.wide)
    for which, weight, grad in ((0, r.w_qkv, r.qkv), (1, r.w_up, r.up)):
        total = jnp.zeros((half, 128), F32)
        for first in range(0, grad.shape[2], 128):
            span = slice(first, first + 128)
            total = total + weight[layer, :, span].astype(F32) * grad[0, :, span]
        r.wide[:half, :] = total
        line = jnp.sum(r.wide[...].T, 0, keepdims=True)[:, :half]
        r.gains_grad[0, which : which + 1, :] = line / r.gains[layer, which : which + 1, :].astype(
            F32
        )


VMEM = pl.BlockSpec(memory_space=pltpu.VMEM)
ANY = pl.BlockSpec(memory_space=pl.ANY)
HBM = pl.BlockSpec(memory_space=pltpu.HBM)


def listed(r, name):
    found = []
    while name + str(len(found)) in vars(r):
        found.append(getattr(r, name + str(len(found))))
    return found


def numbered(name, space, arrays):
    return {name + str(index): (space, array) for index, array in enumerate(arrays)}


def place_here():
    seq = lax.axis_index("seq")
    return (
        jnp.bitwise_and(seq, 1),
        jnp.bitwise_and(lax.shift_right_logical(seq, 1), 1),
        jnp.bitwise_and(lax.shift_right_logical(seq, 2), 3),
        lax.axis_index("fsdp"),
    )


def shape_of(*dims, dtype=BF16):
    return jax.ShapeDtypeStruct(dims, dtype)


def call(kernel, name, ins, outs, scratch, after=(), us=1, vmem=VMEM_LIMIT):
    names = list(ins) + [None] * len(after) + list(outs) + list(scratch)

    def body(*refs):
        named = {n: ref for n, ref in zip(names, refs) if n}
        kernel(types.SimpleNamespace(place=place_here(), **named))

    results = pl.pallas_call(
        body,
        name=name,
        out_shape=list(outs.values()),
        in_specs=[space for space, _ in ins.values()] + [ANY] * len(after),
        out_specs=[VMEM] * len(outs),
        scratch_shapes=list(scratch.values()),
        cost_estimate=pl.CostEstimate(
            flops=1000, bytes_accessed=us * BYTES_PER_US, transcendentals=0
        ),
        compiler_params=pltpu.CompilerParams(vmem_limit_bytes=vmem),
    )(*[array for _, array in ins.values()], *after)
    return types.SimpleNamespace(**dict(zip(outs, results)))


def weight_scratch(first, second, names):
    return {
        names[0]: pltpu.VMEM((2 * first.shape[1], first.shape[2]), BF16),
        names[1]: pltpu.VMEM((2 * second.shape[1], second.shape[2]), BF16),
        names[2]: pltpu.SemaphoreType.DMA((2, 9)),
    }


def attend_weights(weights, parts):
    ins = {"qkv": (HBM, weights[0]), "proj": (HBM, weights[1])} | numbered("a_part", HBM, parts)
    return ins, weight_scratch(weights[0], weights[1], ("qkv_w", "proj_w", "a_sems"))


def mlp_weights(weights, parts):
    ins = {"up": (HBM, weights[2]), "down": (HBM, weights[3])} | numbered("m_part", HBM, parts)
    return ins, weight_scratch(weights[2], weights[3], ("up_w", "down_w", "m_sems"))


def tie(array, after):
    return pl.pallas_call(
        lambda *refs: None,
        name="tie",
        out_shape=jax.ShapeDtypeStruct(array.shape, array.dtype),
        in_specs=[ANY] * (1 + len(after)),
        out_specs=ANY,
        input_output_aliases={0: 0},
        compiler_params=pltpu.CompilerParams(vmem_limit_bytes=1024 * 1024),
    )(array, *after)


def grid_buffer(width, width_c):
    return pltpu.VMEM((WIN, -(-width // 8) * 8, width_c), F32)


def pack(layer, weights, after=()):
    rows = weights[0].shape[1] // 2
    wide = 4 * weights[1].shape[2]
    ins = {
        name: (HBM, w) for name, w in zip(("qkv", "proj", "up", "down"), weights)
    }
    outs = {"both": shape_of(3 * rows, wide)}
    if layer == 0:
        outs = {"attend": shape_of(rows, wide), "mlp": shape_of(2 * rows, wide)}
    scratch = {"sems": pltpu.SemaphoreType.DMA((7,))}
    kernel = functools.partial(pack_kernel, layer)
    limit = PACK_VMEM_LIMIT if layer == 0 else VMEM_LIMIT
    return call(kernel, "pack", ins, outs, scratch, after, vmem=limit)


def pack_small(gains, tables, after=()):
    ins = {"gains": (VMEM, gains), "tables": (VMEM, tables)}
    outs = {"small": shape_of(4 + 2 * tables.shape[1], 2 * gains.shape[2], dtype=F32)}
    return call(pack_small_kernel, "pack_small", ins, outs, {}, after).small


def table_sums(grads, onehot, width_c, after=()):
    heads = grads[0].shape[0]
    rows = heads + -heads % 16
    ins = numbered("grad", VMEM, grads) | {"onehot": (VMEM, onehot)}
    scratch = {"wide": pltpu.VMEM((rows, width_c), F32)}
    outs = {"out": shape_of(rows, width_c)}
    return call(table_sums_kernel, "table_sums", ins, outs, scratch, after).out


def params(own, other, heads):
    width_c = own.shape[1]
    ins = {"own": (VMEM, own), "other": (VMEM, other)}
    outs = {"gains": shape_of(2, 2, width_c, dtype=F32), "table": shape_of(2, heads, TABLE, dtype=F32)}
    return call(params_kernel, "params", ins, outs, {})


def grid_ins(grid, edges=()):
    ins = {"own": (VMEM, grid)}
    if edges:
        ins |= {n: (VMEM, e) for n, e in zip(("rows_in", "cols_in", "corner_in"), edges)}
    return ins


def edge_outs(width, width_c):
    return {
        "rows": shape_of(2, SHIFT, width, width_c),
        "cols": shape_of(2, WIN, SHIFT, width_c),
        "corner": shape_of(2, SHIFT, SHIFT, width_c),
    }


def attend_forward(layer, mode, grid, edges, gains, bias, same, weights, parts, after=()):
    width, width_c = grid.shape[1:]
    tokens = width // WIN * SLOT
    heads = width_c // HEAD
    more, scratch = attend_weights(weights, parts)
    ins = {"gains": (VMEM, gains), "bias": (VMEM, bias)}
    ins |= grid_ins(grid, edges) | more
    if mode != "plain":
        ins |= {"same": (VMEM, same)}
    outs = {
        "x": shape_of(tokens, width_c),
        "middle": shape_of(tokens, width_c, dtype=F32),
        "query_t": shape_of(width_c, tokens),
        "keys_t": shape_of(width_c, tokens),
        "keys": shape_of(tokens, width_c),
        "values": shape_of(tokens, width_c),
        "mixed_t": shape_of(width_c, tokens),
        "probs": shape_of(heads, SLOT, tokens, dtype=F32),
    }
    scratch |= {
        "flat": pltpu.VMEM((tokens, width_c), F32),
        "values_t": pltpu.VMEM((width_c, tokens), BF16),
    }
    kernel = functools.partial(attend_forward_kernel, layer, mode)
    return call(kernel, "attend_forward", ins, outs, scratch, after, 4)


def mlp_forward(layer, middle, gains, weights, parts, top, after=()):
    tokens, width_c = middle.shape
    width = top.shape[1]
    more, scratch = mlp_weights(weights, parts)
    ins = {"middle": (VMEM, middle), "gains": (VMEM, gains)} | more
    ins |= {"top": (VMEM, top)}
    outs = {"grid": shape_of(WIN, width, width_c)} | edge_outs(width, width_c)
    scratch |= {
        "flat": pltpu.VMEM((tokens, width_c), F32),
        "buffer": grid_buffer(width, width_c),
    }
    return call(functools.partial(mlp_forward_kernel, layer), "mlp_forward", ins, outs, scratch, after, 4)


def backward(layer, kept, grid, edges, gains, weights, a_parts, m_parts, after=()):
    tokens, width_c = kept.middle.shape
    width = grid.shape[1]
    heads = width_c // HEAD
    second = layer == 1
    attend_ins, attend_scratch = attend_weights(weights, a_parts)
    mlp_ins, mlp_scratch = mlp_weights(weights, m_parts)
    ins = {"gains": (VMEM, gains)} | grid_ins(grid, edges)
    if second:
        ins["own_two"] = ins.pop("own")
    names = ("middle", "x", "query_t", "keys_t", "values", "probs")
    ins |= {name: (VMEM, getattr(kept, name)) for name in names} | attend_ins | mlp_ins
    pieces = shape_of(2, 2, 2 if second else 3, 4, width_c // 8, width_c)
    outs = {
        "keep": pieces,
        "send": pieces,
        "grad_m": shape_of(tokens, width_c, dtype=F32),
        "grad_t": shape_of(3 * width_c, tokens),
        "bias_grad": shape_of(heads, SLOT, PAIR, dtype=F32),
    }
    scratch = attend_scratch | mlp_scratch
    scratch |= {
        "out_t": pltpu.VMEM((width_c, tokens), BF16),
        "flat": pltpu.VMEM((tokens, width_c), F32),
    }
    if second:
        outs |= {"out": shape_of(WIN, width, width_c), "grid": shape_of(WIN, width, width_c)}
        outs |= edge_outs(width, width_c)
        scratch |= {"buffer": grid_buffer(width, width_c)}
    else:
        ins |= {"mixed_t": (VMEM, kept.mixed_t)}
        scratch |= sides(width_c, tokens)

    def kernel(r):
        mlp_backward_kernel(layer, "in" if second else "out", layer, r)
        attend_backward_kernel(layer, "si" if second else "sw", 2, r)

    return call(kernel, "backward", ins, outs, scratch, after, 15)


def sides(width_c, tokens):
    return {
        "left": pltpu.VMEM((2, width_c, tokens), BF16),
        "right": pltpu.VMEM((4 * width_c, tokens), BF16),
    }


def attend_weight_grads(layer, kept, back, gains, after=()):
    tokens, width_c = back.grad_m.shape
    ins = {"gains": (VMEM, gains), "grad_m": (VMEM, back.grad_m)}
    ins |= {"x": (VMEM, kept.x), "mixed_t": (VMEM, kept.mixed_t), "grad_t": (VMEM, back.grad_t)}
    pieces = shape_of(2, 2, 1, 4, width_c // 8, width_c)
    kernel = functools.partial(attend_backward_kernel, layer, "w", 0)
    outs = {"keep": pieces, "send": pieces}
    return call(kernel, "attend_weight_grads", ins, outs, sides(width_c, tokens), after, 2)


def input_grad(layer, kept, back, gains, weights, a_parts, own_two, edges, after=()):
    tokens, width_c = back.grad_m.shape
    width = own_two.shape[1]
    more, scratch = attend_weights(weights, a_parts)
    ins = {"gains": (VMEM, gains), "grad_m": (VMEM, back.grad_m)}
    ins |= {"x": (VMEM, kept.x), "grad_t": (VMEM, back.grad_t)} | more
    ins |= grid_ins(own_two, edges)
    ins["own_two"] = ins.pop("own")
    outs = {"grid": shape_of(WIN, width, width_c), "mixed": shape_of(WIN, width, width_c)}
    scratch |= {
        "flat": pltpu.VMEM((tokens, width_c), F32),
        "buffer": grid_buffer(width, width_c),
    }

    def kernel(r):
        attend_backward_kernel(layer, "i", 0, r)
        roll_out_kernel(r)

    return call(kernel, "input_grad", ins, outs, scratch, after, 3)


def collect(layer, pieces, weights, gains, into=()):
    names = ("qkv", "proj", "up", "down", "gains_grad")
    grads = [shape_of(*w.shape, dtype=F32) for w in (*weights, gains)]
    arrays = [*pieces, weights[0], weights[2], gains]
    ins = [*["all" + str(i) for i in range(len(pieces))], "w_qkv", "w_up", "gains"]
    scratch = {
        "table": pltpu.VMEM((2, 2, 4, 3, pieces[0].shape[1] // 3, pieces[0].shape[2]), BF16),
        "wide": pltpu.VMEM((256, 128), F32),
    }
    order = ins + [None] * len(into) + list(names) + list(scratch)

    def body(*refs):
        named = {n: r for n, r in zip(order, refs) if n}
        collect_kernel(layer, types.SimpleNamespace(place=place_here(), **named))

    return pl.pallas_call(
        body,
        name="collect",
        grid=(1,),
        out_shape=grads,
        in_specs=[VMEM] * len(arrays) + [ANY] * len(into),
        out_specs=[pl.BlockSpec((1, *g.shape[1:]), lambda i: (layer, 0, 0)) for g in grads],
        scratch_shapes=list(scratch.values()),
        input_output_aliases={len(arrays) + i: i for i in range(len(into))},
        compiler_params=pltpu.CompilerParams(vmem_limit_bytes=VMEM_LIMIT),
    )(*arrays, *into)


def same_label(labels):
    same = labels[:, :, None] == labels[:, None, :]
    return same.astype(F32).transpose(1, 0, 2).reshape(SLOT, -1)


def per_device(
    tokens, norm_gains, w_qkv, w_proj, w_up, w_down, tables, region_ids, rel_index, cotangent
):
    y = lax.axis_index("fsdp")
    width, width_c = tokens.shape[1:]
    weights = (w_qkv, w_proj, w_up, w_down)

    heads = 2 * tables.shape[1]

    piece = pack(0, weights)
    small = pack_small(norm_gains, tables, after=(piece.attend,))
    settings = params(small, exchange(small, 0, 1), heads)
    gains = settings.gains
    attend_one = share_halves(piece.attend)
    mlp_piece = tie(piece.mlp, (small,))
    index = rel_index.reshape(WIN, WIN, WIN, WIN)
    index = jnp.pad(index, [(0, 1)] * 4, constant_values=-1).reshape(SLOT, SLOT).T
    index = jnp.concatenate([index, index], axis=1)
    onehot = (index[:, :, None] == jnp.arange(TABLE, dtype=jnp.int32)).astype(BF16)
    bias = jnp.einsum(
        "lht,jit->lhji", settings.table.astype(BF16), onehot, preferred_element_type=F32
    )
    labels = region_ids.reshape(WIN, width // WIN, WIN).transpose(1, 0, 2)
    labels = jnp.pad(labels, [(0, 0), (0, 1), (0, 1)], constant_values=-1)
    same = same_label(labels.reshape(-1, SLOT))
    piece = pack(1, weights, after=(gains, bias, same))
    one = attend_forward(
        0, "plain", tokens, (), gains, bias, None, weights, attend_one, after=(piece.both,)
    )
    mlp_one = share_halves(mlp_piece, after=(one.middle,))
    done = mlp_forward(0, one.middle, gains, weights, mlp_one, cotangent)
    edges = halo(done.rows, done.cols, done.corner, 1)
    parts_two = share_halves(piece.both, after=edges)
    two = attend_forward(
        1, "in", done.grid, edges, gains, bias, same, weights, parts_two
    )
    back2 = backward(1, two, cotangent, edges, gains, weights, parts_two, parts_two)
    got_m2 = exchange(back2.send, 1, 0)
    edges = halo(back2.rows, back2.cols, back2.corner, -1)
    att2 = attend_weight_grads(1, two, back2, gains)
    side_two = start_side(
        (back2.keep, att2.keep), (got_m2, exchange(att2.send, 1, 0)), after=edges
    )
    back1 = backward(
        0, one, back2.grid, edges, gains, weights, attend_one, mlp_one, after=(side_two[0],)
    )
    face_two = start_face(side_two, after=(back1.grad_m,))
    rows = width_c // 8
    small = table_sums((back1.bias_grad, back2.bias_grad), onehot, width_c, after=face_two[:1])
    cube_one = start_cube(
        back1.keep, exchange(tie(back1.send, face_two[:1]), 1, 0), (small, exchange(small, 1, 0))
    )
    last = input_grad(
        0, one, back1, gains, weights, attend_one, back2.out, edges, after=cube_one[:1]
    )
    total_two = finish_sum(face_two, rows, after=(last.mixed,))
    total_one = finish_sum(cube_one, rows, after=(total_two,))
    all_two = gather(total_two, 3 * rows)
    all_one = gather(total_one, 3 * rows, after=all_two[:1])
    sums = collect(1, all_two, weights, norm_gains)
    sums = collect(0, all_one, weights, norm_gains, into=sums)
    small = total_one[3 * rows : 3 * rows + heads].astype(F32).reshape(heads, 2, width_c // 2)
    small = small[:, :, :TABLE].transpose(1, 0, 2)
    tables_grad = lax.dynamic_slice_in_dim(small, y * (heads // 2), heads // 2, axis=1)
    return (last.mixed, last.grid, sums[4], *sums[:4], tables_grad)


def solution(mesh):
    return jax.shard_map(
        per_device,
        mesh=mesh,
        in_specs=(
            P("seq", "fsdp", None),
            P(None, None, "fsdp"),
            P(None, "fsdp", None),
            P(None, "fsdp", None),
            P(None, "fsdp", None),
            P(None, "fsdp", None),
            P(None, "fsdp", None),
            P("seq", "fsdp"),
            P(),
            P("seq", "fsdp", None),
        ),
        out_specs=(
            P("seq", "fsdp", None),
            P("seq", "fsdp", None),
            P(None, None, "fsdp"),
            P(None, "fsdp", None),
            P(None, "fsdp", None),
            P(None, "fsdp", None),
            P(None, "fsdp", None),
            P(None, "fsdp", None),
        ),
        check_vma=False,
    )
```

time: 554 us -> 185 us (0.33); the launches traced: 544 us -> 184 us
  waiting for transfers between devices: 280 us -> 73.7 us
  blocking collectives: 93.2 us -> 0 us
  matrix products: 53.5 us -> 1.76 us
  Pallas kernels: 0 us -> 47.5 us
  local copies, waits for them, and re-layouts: 46.1 us -> 8.34 us
  other arithmetic: 36.7 us -> 2.15 us
  starting transfers between devices: 17.1 us -> 49.7 us
  between operations: 16.8 us -> 1.1 us
    reduce_scatter x8 -> x0, waiting for transfers between devices: 107 us -> none  [the longest x1 22.6 us: per_device(): lax.psum_scatter(grads_two[3].astype(jnp.bfloat16), 'fsdp', scatter_dimen...]
    psum x1 -> x0, waiting for transfers between devices: 92.4 us -> none  [per_device(): lax.psum((shards[0], shards[1], shards[2], shards[3], shards[4], shards[5...]
    psum x1 -> x0, blocking collectives: 63.5 us -> none  [per_device(): lax.psum((shards[0], shards[1], shards[2], shards[3], shards[4], shards[5...]
    all_gather x3 -> x0, waiting for transfers between devices: 61.9 us -> none  [the longest x1 34.8 us: per_device(): lax.all_gather(w_down, 'fsdp', axis=1, tiled=True)]
    ppermute x8 -> x46, waiting for transfers between devices: 12.8 us -> 73.7 us  [the longest x40 67.7 us: exchange(): return lax.ppermute(array, ('seq', 'fsdp'), pairs)]
    dot_general x40 -> x1, matrix products: 53.5 us -> 1.76 us  [per_device(): jnp.einsum('lht,jit->lhji', settings.table.astype(BF16), onehot, preferre...]
    pallas_call x0 -> x25, Pallas kernels: none -> 47.5 us  [the longest x19 40.5 us: call(): pl.pallas_call(body, name=name, out_shape=list(outs.values()), in_specs=[...]
    ppermute x8 -> x46, starting transfers between devices: 12.6 us -> 49.7 us  [the longest x40 40.1 us: exchange(): return lax.ppermute(array, ('seq', 'fsdp'), pairs)]
  transfers between devices with their start and end apart: 24 -> 46, of which waited for: 14 -> 23; matrix products, arithmetic and copies ran while one was open for 16% -> 3% of each run, Pallas kernels for 0% -> 14%
where the time goes in v1:
time: 185 us; the launch traced here: 184 us
  waiting for transfers between devices  73.7 us (40%)
  starting transfers between devices  49.7 us (27%)
  Pallas kernels  47.5 us (26%)
  local copies, waits for them, and re-layouts  8.34 us (5%)
  other arithmetic  2.15 us (1%)
    ppermute x40, waiting for transfers between devices, exchange(): return lax.ppermute(array, ('seq', 'fsdp'), pairs)  67.7 us
    pallas_call x19, Pallas kernels, call(): pl.pallas_call(body, name=name, out_shape=list(outs.values()), in_specs=[...  40.5 us
    ppermute x40, starting transfers between devices, exchange(): return lax.ppermute(array, ('seq', 'fsdp'), pairs)  40.1 us
    ppermute x6, starting transfers between devices, take_from(): return lax.ppermute(array, ('seq', 'fsdp'), pairs)  9.6 us
    unnamed x37, local copies, waits for them, and re-layouts  7.06 us
    pallas_call x2, Pallas kernels, collect(): pl.pallas_call(body, name='collect', grid=(1,), out_shape=grads, in_specs...  6.92 us
    ppermute x6, waiting for transfers between devices, take_from(): return lax.ppermute(array, ('seq', 'fsdp'), pairs)  5.95 us
  transfers between devices with their start and end apart: 46, of which 23 were waited for; matrix products, arithmetic and copies ran while one was open for 3% of the time, Pallas kernels for 14%

profile of v1, /device:TPU:0, one launch (start us, length us, event | category | flops | bytes accessed | tf_op | source)
XLA Modules:
  0.0 184.2 jit_solution(7467326170036295735)
XLA Ops:
  0.7 2.2 %pack.2 = (bf16[96,1536]{1,0:T(8,128)(2,1)}, bf16[192,1536]{1,0:T(8,128)(2,1)}) custom-call(bf16[2,192,1152]{2,1,0:T(8,128)(2,1)} %refs_8_.3, bf16[2,192,384]{2,1,0:T(8,128)(2,1)} %refs_5_.1, bf16[2,192,1536]{2,1,0:T(8,128)(2,1)} %refs_9_.3, bf16[2,768,384]{2,1,0:T(8,128)(2,1)} %refs_16_.3), custom_call_target="tpu_custom_call" | custom-call | flops 1000 | bytes 3500000 | tf_op jit(solution)/shard_map/pack/pallas_call | solution.py:667
  2.9 3.0 %collective-permute-start.1 = (bf16[96,1536]{1,0:T(8,128)(2,1)}, bf16[96,1536]{1,0:T(8,128)(2,1)S(1)}, u32[]{:S(2)}, u32[]{:S(2)}) collective-permute-start(bf16[96,1536]{1,0:T(8,128)(2,1)} %get-tuple-element.77.refs_2_), channel_id=1, source_target_pairs={{0,1},{1,0},{2,3},{3,2},{4,5},{5,4},{6,7},{7,6},{8,9},{9,8},{10,11... | collective-permute-start | bytes 884744 | tf_op jit(solution)/shard_map/ppermute | solution.py:30
  5.9 1.0 copy-done.7
  6.9 1.1 copy-done.5
  8.0 0.8 copy-done.6
  8.8 2.0 %collective-permute-start.3 = (bf16[192,1536]{1,0:T(8,128)(2,1)}, bf16[192,1536]{1,0:T(8,128)(2,1)S(1)}, u32[]{:S(2)}, u32[]{:S(2)}) collective-permute-start(bf16[192,1536]{1,0:T(8,128)(2,1)} %copy-done.6), channel_id=1, source_target_pairs={{0,1},{1,0},{2,3},{3,2},{4,5},{5,4},{6,7},{7,6},{8,9},{9,8},{10,11... | collective-permute-start | bytes 1769480 | tf_op jit(solution)/shard_map/ppermute | solution.py:30
  11.9 2.6 %collective-permute-done.refs_1_ = f32[16,384]{1,0:T(8,128)S(1)} collective-permute-done((f32[16,384]{1,0:T(8,128)S(1)}, f32[16,384]{1,0:T(8,128)S(1)}, u32[]{:S(2)}, u32[]{:S(2)}) %collective-permute-start) | collective-permute-done | bytes 24608 | tf_op jit(solution)/shard_map/ppermute | solution.py:30
  14.6 1.8 fusion.2
  16.9 2.1 %collective-permute-start.8 = (bf16[288,1536]{1,0:T(8,128)(2,1)S(1)}, bf16[288,1536]{1,0:T(8,128)(2,1)S(1)}, u32[]{:S(2)}, u32[]{:S(2)}) collective-permute-start(bf16[288,1536]{1,0:T(8,128)(2,1)S(1)} %pack.3.refs_7_), channel_id=1, source_target_pairs={{0,1},{1,0},{2,3},{3,2},{4,5},{5,4},{6,7},{7,6},{8,9},{9,8},{10,11... | collective-permute-start | bytes 2654216 | tf_op jit(solution)/shard_map/ppermute | solution.py:30
  19.1 2.8 %attend_forward.2 = (bf16[256,384]{1,0:T(8,128)(2,1)S(1)}, f32[256,384]{1,0:T(8,128)S(1)}, bf16[384,256]{1,0:T(8,128)(2,1)S(1)}, bf16[384,256]{1,0:T(8,128)(2,1)...) custom-call(f32[2,2,384]{2,1,0:T(2,128)S(1)} %get-tuple-element.78.r, ...), custom_call_target="tpu_custom_call" | custom-call | flops 1000 | bytes 14000000 | tf_op jit(solution)/shard_map/attend_forward/pallas_call | solution.py:667
  21.9 5.3 %collective-permute-done.3.refs_0_ = bf16[192,1536]{1,0:T(8,128)(2,1)S(1)} collective-permute-done((bf16[192,1536]{1,0:T(8,128)(2,1)}, bf16[192,1536]{1,0:T(8,128)(2,1)S(1)}, u32[]{:S(2)}, u32[]{:S(2)}) %collective-permute-start.3) | collective-permute-done | bytes 589856 | tf_op jit(solution)/shard_map/ppermute | solution.py:30
  27.1 2.0 %collective-permute-done.4.refs_5_.refs_18_ = bf16[192,1536]{1,0:T(8,128)(2,1)S(1)} collective-permute-done((bf16[192,1536]{1,0:T(8,128)(2,1)S(1)}, bf16[192,1536]{1,0:T(8,128)(2,1)S(1)}, u32[]{:S(2)}, u32[]{:S(2)}) %collective-permute-start.4) | collective-permute-done | bytes 589856 | tf_op jit(solution)/shard_map/ppermute | solution.py:30
  29.1 2.6 %mlp_forward.1 = (bf16[7,28,384]{2,1,0:T(8,128)(2,1)S(1)}, bf16[2,3,28,384]{3,2,1,0:T(8,128)(2,1)S(1)}, bf16[2,7,3,384]{3,2,1,0:T(4,128)(2,1)S(1)}, bf16[2,3,3,384]{3,2,1,0:T(4,128)(2,1)S(1)}) custom-call(f32[256,384]{1,0:T(8,128)S(1)} %get-tuple-element.80.refs_1_.refs_0_.refs_5_, f32[2,2,384]{2,1,0:T(2,128)S(1)} %get-tuple-element.78.refs_4_.refs_0_.refs_1_, ...), custom_call_target="tpu_custom_call" | custom-call | flops 1000 | bytes 14000000 | tf_op jit(solution)/shard_map/mlp_forward/pallas_call | solution.py:667
  31.7 4.9 %collective-permute-start.5 = (bf16[2,3,28,384]{3,2,1,0:T(8,128)(2,1)S(1)}, bf16[2,3,28,384]{3,2,1,0:T(8,128)(2,1)S(1)}, u32[]{:S(2)}, u32[]{:S(2)}) collective-permute-start(bf16[2,3,28,384]{3,2,1,0:T(8,128)(2,1)S(1)} %get-tuple-element.82), channel_id=1, source_target_pairs={{2,0},{3,1},{4,2},{5,3},{6,4},{7,5},{8,6},{9,7},{10,8},{11,9},{12,... | collective-permute-start | bytes 387080 | tf_op jit(solution)/shard_map/ppermute | solution.py:36
  36.6 1.5 collective-permute-start.6
  38.1 8.0 %collective-permute-done.8.refs_0_ = bf16[288,1536]{1,0:T(8,128)(2,1)S(1)} collective-permute-done((bf16[288,1536]{1,0:T(8,128)(2,1)S(1)}, bf16[288,1536]{1,0:T(8,128)(2,1)S(1)}, u32[]{:S(2)}, u32[]{:S(2)}) %collective-permute-start.8) | collective-permute-done | bytes 884768 | tf_op jit(solution)/shard_map/ppermute | solution.py:30
  46.6 2.4 %collective-permute-done.9.refs_9_.refs_14_.refs_18_ = bf16[288,1536]{1,0:T(8,128)(2,1)S(1)} collective-permute-done((bf16[288,1536]{1,0:T(8,128)(2,1)S(1)}, bf16[288,1536]{1,0:T(8,128)(2,1)S(1)}, u32[]{:S(2)}, u32[]{:S(2)}) %collective-permute-start.9) | collective-permute-done | bytes 884768 | tf_op jit(solution)/shard_map/ppermute | solution.py:30
  49.0 2.8 %attend_forward.3 = (bf16[256,384]{1,0:T(8,128)(2,1)S(1)}, f32[256,384]{1,0:T(8,128)S(1)}, bf16[384,256]{1,0:T(8,128)(2,1)S(1)}, bf16[384,256]{1,0:T(8,128)(2,1)...) custom-call(f32[2,2,384]{2,1,0:T(2,128)S(1)} %get-tuple-element.78.r, ...), custom_call_target="tpu_custom_call" | custom-call | flops 1000 | bytes 14000000 | tf_op jit(solution)/shard_map/attend_forward/pallas_call | solution.py:667
  51.8 12.3 %backward.2 = (bf16[2,2,2,4,48,384]{5,4,3,2,1,0:T(8,128)(2,1)S(1)}, bf16[2,2,2,4,48,384]{5,4,3,2,1,0:T(8,128)(2,1)S(1)}, f32[256,384]{1,0:T(8,128)S(1)}, bf16[11...) custom-call(f32[2,2,384]{2,1,0:T(2,128)S(1)} %get-tuple-element.78.r, ...), custom_call_target="tpu_custom_call" | custom-call | flops 1000 | bytes 52500000 | tf_op jit(solution)/shard_map/backward/pallas_call | solution.py:667
  64.4 0.9 attend_weight_grads.1
  65.8 1.7 collective-permute-start.11
  67.6 1.3 collective-permute-start.12
  68.9 5.5 %collective-permute-done.12.refs_6_.refs_4_.refs_10_ = bf16[2,3,3,384]{3,2,1,0:T(4,128)(2,1)S(1)} collective-permute-done((bf16[2,3,3,384]{3,2,1,0:T(4,128)(2,1)S(1)}, bf16[2,3,3,384]{3,2,1,0:T(4,128)(2,1)S(1)}, u32[]{:S(2)}, u32[]{:S(2)}) %collective-permute-start.12) | collective-permute-done | bytes 13856 | tf_op jit(solution)/shard_map/ppermute | solution.py:36
  75.2 11.6 %backward.3 = (bf16[2,2,3,4,48,384]{5,4,3,2,1,0:T(8,128)(2,1)S(1)}, bf16[2,2,3,4,48,384]{5,4,3,2,1,0:T(8,128)(2,1)S(1)}, f32[256,384]{1,0:T(8,128)S(1)}, bf16[1152,256]{1,0:T(8,128)(2,1)S(1)}, f32[12,64,128]{2,1,0:T(8,128)S(1)}) custom-call(f32[2,2,384]{2,1,0:T(2,128)S(1)} %get-tuple-element.78.refs_4_.refs_0_.refs_1_, ...), custom_call_target="tpu_custom_call" | custom-call | flops 1000 | bytes 52500000 | tf_op jit(solution)/shard_map/backward/pallas_call | solution.py:667
  86.8 7.5 %collective-permute-done.15.refs_1_ = bf16[2,3,4,48,384]{4,3,2,1,0:T(8,128)(2,1)S(1)} collective-permute-done((bf16[2,3,4,48,384]{4,3,2,1,0:T(8,128)(2,1)S(1)}, bf16[2,3,4,48,384]{4,3,2,1,0:T(8,128)(2,1)S(1)}, u32[]{:S(2)}, u32[]{:S(2)}) %collective-permute-start.15) | collective-permute-done | bytes 884768 | tf_op jit(solution)/shard_map/ppermute | solution.py:30
  94.6 2.3 %collective-permute-start.25 = (bf16[288,384]{1,0:T(8,128)(2,1)S(1)}, bf16[288,384]{1,0:T(8,128)(2,1)S(1)}, u32[]{:S(2)}, u32[]{:S(2)}) collective-permute-start(bf16[288,384]{1,0:T(8,128)(2,1)S(1)} %get-tuple-element.129), channel_id=1, source_target_pairs={{0,12},{1,13},{2,14},{3,15},{4,8},{5,9},{6,10},{7,11},{8,4},{9,5},... | collective-permute-start | bytes 663560 | tf_op jit(solution)/shard_map/ppermute | solution.py:30
  96.9 0.8 collective-permute-start.26
  98.2 1.4 fusion.refs_2_
  99.6 1.0 table_sums.1.refs_2_
  100.6 1.2 collective-permute-done.17.refs_3_
  102.2 2.3 %collective-permute-start.18 = (bf16[304,384]{1,0:T(8,128)(2,1)S(1)}, bf16[304,384]{1,0:T(8,128)(2,1)S(1)}, u32[]{:S(2)}, u32[]{:S(2)}) collective-permute-start(bf16[304,384]{1,0:T(8,128)(2,1)S(1)} %get-tuple-element.122), channel_id=1, source_target_pairs={{0,13},{1,12},{2,15},{3,14},{4,9},{5,8},{6,11},{7,10},{8,5},{9,4},... | collective-permute-start | bytes 700424 | tf_op jit(solution)/shard_map/ppermute | solution.py:30
  104.5 1.7 collective-permute-start.19
  106.2 2.6 %input_grad.1 = (bf16[7,28,384]{2,1,0:T(8,128)(2,1)}, bf16[7,28,384]{2,1,0:T(8,128)(2,1)}) custom-call(f32[2,2,384]{2,1,0:T(2,128)S(1)} %get-tuple-element.78.refs_4_.refs_0_.refs_1_, f32[256,384]{1,0:T(8,128)S(1)} %get-tuple-element.110.refs_2_.refs_1_, bf16[256,384]{1,0:T(8,128)(2,1)S(1)} %get-tuple-element.96.refs_6_.refs_2_, ...), custom_call_target="tpu_custom_call" | custom-call | flops 1000 | bytes 10500000 | tf_op jit(solution)/shard_map/input_grad/pallas_call | solution.py:667
  108.9 0.9 copy-done.12
  109.9 2.7 %collective-permute-start.28 = (bf16[144,384]{1,0:T(8,128)(2,1)S(1)}, bf16[144,384]{1,0:T(8,128)(2,1)S(1)}, u32[]{:S(2)}, u32[]{:S(2)}) collective-permute-start(bf16[144,384]{1,0:T(8,128)(2,1)S(1)} %get-tuple-element.133), channel_id=1, source_target_pairs={{0,16},{1,17},{2,18},{3,19},{4,20},{5,21},{6,22},{7,23},{8,24},{9,... | collective-permute-start | bytes 331784 | tf_op jit(solution)/shard_map/ppermute | solution.py:30
  112.6 1.3 collective-permute-start.20
  113.9 1.5 collective-permute-start.21
  115.4 2.6 %collective-permute-done.28 = bf16[144,384]{1,0:T(8,128)(2,1)S(1)} collective-permute-done((bf16[144,384]{1,0:T(8,128)(2,1)S(1)}, bf16[144,384]{1,0:T(8,128)(2,1)S(1)}, u32[]{:S(2)}, u32[]{:S(2)}) %collective-permute-start.28) | collective-permute-done | bytes 110624 | tf_op jit(solution)/shard_map/ppermute | solution.py:30
  118.0 0.9 collective-permute-start.22
  118.9 1.0 collective-permute-start.23
  120.2 1.8 %collective-permute-start.24 = (bf16[304,384]{1,0:T(8,128)(2,1)S(1)}, bf16[304,384]{1,0:T(8,128)(2,1)S(1)}, u32[]{:S(2)}, u32[]{:S(2)}) collective-permute-start(bf16[304,384]{1,0:T(8,128)(2,1)S(1)} %get-tuple-element.128), channel_id=1, source_target_pairs={{0,8},{1,9},{2,10},{3,11},{4,12},{5,13},{6,14},{7,15},{8,0},{9,1},... | collective-permute-start | bytes 700424 | tf_op jit(solution)/shard_map/ppermute | solution.py:30
  122.1 2.0 %collective-permute-done.20.refs_3_ = bf16[304,384]{1,0:T(8,128)(2,1)S(1)} collective-permute-done((bf16[304,384]{1,0:T(8,128)(2,1)S(1)}, bf16[304,384]{1,0:T(8,128)(2,1)S(1)}, u32[]{:S(2)}, u32[]{:S(2)}) %collective-permute-start.20) | collective-permute-done | bytes 233504 | tf_op jit(solution)/shard_map/ppermute | solution.py:30
  124.2 3.7 %collective-permute-done.21.refs_4_ = bf16[304,384]{1,0:T(8,128)(2,1)S(1)} collective-permute-done((bf16[304,384]{1,0:T(8,128)(2,1)S(1)}, bf16[304,384]{1,0:T(8,128)(2,1)S(1)}, u32[]{:S(2)}, u32[]{:S(2)}) %collective-permute-start.21) | collective-permute-done | bytes 233504 | tf_op jit(solution)/shard_map/ppermute | solution.py:30
  127.8 1.8 collective-permute-done.22.refs_5_
  129.6 0.8 collective-permute-done.23.refs_6_
  130.4 2.7 %collective-permute-done.24.refs_7_ = bf16[304,384]{1,0:T(8,128)(2,1)S(1)} collective-permute-done((bf16[304,384]{1,0:T(8,128)(2,1)S(1)}, bf16[304,384]{1,0:T(8,128)(2,1)S(1)}, u32[]{:S(2)}, u32[]{:S(2)}) %collective-permute-start.24) | collective-permute-done | bytes 233504 | tf_op jit(solution)/shard_map/ppermute | solution.py:30
  133.3 2.8 %collective-permute-start.29 = (bf16[160,384]{1,0:T(8,128)(2,1)S(1)}, bf16[160,384]{1,0:T(8,128)(2,1)S(1)}, u32[]{:S(2)}, u32[]{:S(2)}) collective-permute-start(bf16[160,384]{1,0:T(8,128)(2,1)S(1)} %get-tuple-element.135), channel_id=1, source_target_pairs={{0,16},{1,17},{2,18},{3,19},{4,20},{5,21},{6,22},{7,23},{8,24},{9,... | collective-permute-start | bytes 368648 | tf_op jit(solution)/shard_map/ppermute | solution.py:30
  136.3 10.4 %collective-permute-done.31.refs_1_ = bf16[144,384]{1,0:T(8,128)(2,1)S(1)} collective-permute-done((bf16[144,384]{1,0:T(8,128)(2,1)S(1)}, bf16[144,384]{1,0:T(8,128)(2,1)S(1)}, u32[]{:S(2)}, u32[]{:S(2)}) %collective-permute-start.31) | collective-permute-done | bytes 110624 | tf_op jit(solution)/shard_map/ppermute | solution.py:30
  147.0 1.7 collective-permute-start.40
  148.7 1.6 collective-permute-start.39
  150.4 1.8 collective-permute-start.30
  152.2 6.5 %collective-permute-done.41.refs_3_ = bf16[2,144,384]{2,1,0:T(8,128)(2,1)S(1)} collective-permute-done((bf16[2,144,384]{2,1,0:T(8,128)(2,1)S(1)}, bf16[2,144,384]{2,1,0:T(8,128)(2,1)S(1)}, u32[]{:S(2)}, u32[]{:S(2)}) %collective-permute-start.41) | collective-permute-done | bytes 221216 | tf_op jit(solution)/shard_map/ppermute | solution.py:30
  158.7 0.7 collective-permute-done.40.refs_2_
  159.8 4.0 %collective-permute-start.34 = (bf16[2,144,384]{2,1,0:T(8,128)(2,1)S(1)}, bf16[2,144,384]{2,1,0:T(8,128)(2,1)}, u32[]{:S(2)}, u32[]{:S(2)}) collective-permute-start(bf16[2,144,384]{2,1,0:T(8,128)(2,1)S(1)} %stack.3.refs_0_), channel_id=1, source_target_pairs={{0,12},{1,13},{2,14},{3,15},{4,8},{5,9},{6,10},{7,11},{8,4},{9,5},... | collective-permute-start | bytes 663560 | tf_op jit(solution)/shard_map/ppermute | solution.py:30
  163.9 1.7 collective-permute-start.33
  165.6 0.7 copy-done.8
  166.3 0.7 copy-done.10
  167.5 2.8 %collective-permute-done.34.refs_3_ = bf16[2,144,384]{2,1,0:T(8,128)(2,1)} collective-permute-done((bf16[2,144,384]{2,1,0:T(8,128)(2,1)S(1)}, bf16[2,144,384]{2,1,0:T(8,128)(2,1)}, u32[]{:S(2)}, u32[]{:S(2)}) %collective-permute-start.34) | collective-permute-done | bytes 221216 | tf_op jit(solution)/shard_map/ppermute | solution.py:30
  170.3 3.9 %collective-permute-done.33.refs_2_ = bf16[2,144,384]{2,1,0:T(8,128)(2,1)} collective-permute-done((bf16[2,144,384]{2,1,0:T(8,128)(2,1)S(1)}, bf16[2,144,384]{2,1,0:T(8,128)(2,1)}, u32[]{:S(2)}, u32[]{:S(2)}) %collective-permute-start.33) | collective-permute-done | bytes 221216 | tf_op jit(solution)/shard_map/ppermute | solution.py:30
  174.8 0.6 convert_bitcast_fusion
  175.4 0.9 copy-done.9
  176.3 0.9 copy-done.11
  177.3 3.2 %collect.2 = (f32[2,192,1152]{2,1,0:T(8,128)}, f32[2,192,384]{2,1,0:T(8,128)}, f32[2,192,1536]{2,1,0:T(8,128)}, f32[2,768,384]{2,1,0:T(8,128)}, f32[2,2,192]{2,1,0:T(2,128)}) custom-call(bf16[2,144,384]{2,1,0:T(8,128)(2,1)S(1)} %stack.2.refs_2_.refs_0_, bf16[2,144,384]{2,1,0:T(8,128)(2,1)S(1)} %collective-permute-done.39.refs_1_, ...), custom_call_target="tpu_custom_call" | custom-call | tf_op jit(solution)/shard_map/collect/pallas_call | solution.py:902
  180.5 3.7 %collect.3 = (f32[2,192,1152]{2,1,0:T(8,128)}, f32[2,192,384]{2,1,0:T(8,128)}, f32[2,192,1536]{2,1,0:T(8,128)}, f32[2,768,384]{2,1,0:T(8,128)}, f32[2,2,192]{2,1,0:T(2,128)}) custom-call(bf16[2,144,384]{2,1,0:T(8,128)(2,1)S(1)} %stack.3.refs_0_, ...), custom_call_target="tpu_custom_call", output_to_operand_aliasing={{0}: (11, {}), {1}: (12, {}), {2}: (13, {}), {3}: (14, {}),... | custom-call | tf_op jit(solution)/shard_map/collect/pallas_call | solution.py:902
  (112 shorter events, 8.0 us)
Async XLA Ops:
  0.6 5.3 %copy-start.16 = (bf16[2,6,169]{2,0,1:T(2,128)(2,1)S(1)}, bf16[2,6,169]{2,0,1:T(2,128)(2,1)}, u32[]{:S(2)}) copy-start(bf16[2,6,169]{2,0,1:T(2,128)(2,1)} %param.16) | copy-start | bytes 12172
  0.6 5.3 %copy-start.14 = (bf16[2,2,192]{2,1,0:T(2,128)(2,1)S(1)}, bf16[2,2,192]{2,1,0:T(2,128)(2,1)}, u32[]{:S(2)}) copy-start(bf16[2,2,192]{2,1,0:T(2,128)(2,1)} %refs_10_.3) | copy-start | bytes 4612
  0.7 10.2 %copy-start.17 = (s32[7,28]{1,0:T(8,128)S(1)}, s32[7,28]{1,0:T(8,128)}, u32[]{:S(2)}) copy-start(s32[7,28]{1,0:T(8,128)} %param.17) | copy-start | bytes 2356
  0.7 10.8 %copy-start.15 = (s32[49,49]{1,0:T(8,128)S(1)}, s32[49,49]{1,0:T(8,128)}, u32[]{:S(2)}) copy-start(s32[49,49]{1,0:T(8,128)} %param.18) | copy-start | bytes 28816
  2.9 11.7 %collective-permute-start.1 = (bf16[96,1536]{1,0:T(8,128)(2,1)}, bf16[96,1536]{1,0:T(8,128)(2,1)S(1)}, u32[]{:S(2)}, u32[]{:S(2)}) collective-permute-start(bf16[96,1536]{1,0:T(8,128)(2,1)} %get-tuple-element.77.refs_2_), channel_id=1, source_target_pairs={{0,1},{1,0},{2,3},{3,2},{4,5},{5,4},{6,7},{7,6},{8,9},{9,8},{10,11... | collective-permute-start | bytes 884744 | tf_op jit(solution)/shard_map/ppermute | solution.py:30
  5.9 1.0 copy-start.7
  6.9 7.6 %collective-permute-start = (f32[16,384]{1,0:T(8,128)S(1)}, f32[16,384]{1,0:T(8,128)S(1)}, u32[]{:S(2)}, u32[]{:S(2)}) collective-permute-start(f32[16,384]{1,0:T(8,128)S(1)} %pack_small.1.refs_0_.refs_1_), channel_id=1, source_target_pairs={{0,1},{1,0},{2,3},{3,2},{4,5},{5,4},{6,7},{7,6},{8,9},{9,8},{10,11... | collective-permute-start | bytes 73736 | tf_op jit(solution)/shard_map/ppermute | solution.py:30
  6.9 1.1 copy-start.5
  8.0 0.8 copy-start.6
  8.8 18.3 %collective-permute-start.3 = (bf16[192,1536]{1,0:T(8,128)(2,1)}, bf16[192,1536]{1,0:T(8,128)(2,1)S(1)}, u32[]{:S(2)}, u32[]{:S(2)}) collective-permute-start(bf16[192,1536]{1,0:T(8,128)(2,1)} %copy-done.6), channel_id=1, source_target_pairs={{0,1},{1,0},{2,3},{3,2},{4,5},{5,4},{6,7},{7,6},{8,9},{9,8},{10,11... | collective-permute-start | bytes 1769480 | tf_op jit(solution)/shard_map/ppermute | solution.py:30
  14.6 4.5 %collective-permute-start.2 = (bf16[96,1536]{1,0:T(8,128)(2,1)S(1)}, bf16[96,1536]{1,0:T(8,128)(2,1)S(1)}, u32[]{:S(2)}, u32[]{:S(2)}) collective-permute-start(bf16[96,1536]{1,0:T(8,128)(2,1)S(1)} %collective-permute-done.1.refs_5_.refs_13_.refs_6_), channel_id=1, source_target_pairs={{0,2},{1,3},{2,0},{3,1},{4,6},{5,7},{6,4},{7,5},{8,10},{9,11},{10,... | collective-permute-start | bytes 884744 | tf_op jit(solution)/shard_map/ppermute | solution.py:30
  14.6 2.1 %copy-start = (bf16[2,192,1152]{2,1,0:T(8,128)(2,1)S(1)}, bf16[2,192,1152]{2,1,0:T(8,128)(2,1)}, u32[]{:S(2)}) copy-start(bf16[2,192,1152]{2,1,0:T(8,128)(2,1)} %refs_8_.3) | copy-start | bytes 2654212
  14.6 2.1 %copy-start.1 = (bf16[2,192,1536]{2,1,0:T(8,128)(2,1)S(1)}, bf16[2,192,1536]{2,1,0:T(8,128)(2,1)}, u32[]{:S(2)}) copy-start(bf16[2,192,1536]{2,1,0:T(8,128)(2,1)} %refs_9_.3) | copy-start | bytes 3538948
  14.6 2.1 %copy-start.2 = (bf16[2,768,384]{2,1,0:T(8,128)(2,1)S(1)}, bf16[2,768,384]{2,1,0:T(8,128)(2,1)}, u32[]{:S(2)}) copy-start(bf16[2,768,384]{2,1,0:T(8,128)(2,1)} %refs_16_.3) | copy-start | bytes 3538948
  14.6 2.1 %copy-start.3 = (bf16[2,192,384]{2,1,0:T(8,128)(2,1)S(1)}, bf16[2,192,384]{2,1,0:T(8,128)(2,1)}, u32[]{:S(2)}) copy-start(bf16[2,192,384]{2,1,0:T(8,128)(2,1)} %refs_5_.1) | copy-start | bytes 884740
  16.7 2.4 %copy-start.13 = (bf16[7,28,384]{2,1,0:T(8,128)(2,1)S(1)}, bf16[7,28,384]{2,1,0:T(8,128)(2,1)}, u32[]{:S(2)}) copy-start(bf16[7,28,384]{2,1,0:T(8,128)(2,1)} %refs_2_.6) | copy-start | bytes 451588
  16.9 12.2 %copy-start.4 = (bf16[7,28,384]{2,1,0:T(8,128)(2,1)S(1)}, bf16[7,28,384]{2,1,0:T(8,128)(2,1)}, u32[]{:S(2)}) copy-start(bf16[7,28,384]{2,1,0:T(8,128)(2,1)} %refs_4_.4) | copy-start | bytes 451588
  16.9 29.2 %collective-permute-start.8 = (bf16[288,1536]{1,0:T(8,128)(2,1)S(1)}, bf16[288,1536]{1,0:T(8,128)(2,1)S(1)}, u32[]{:S(2)}, u32[]{:S(2)}) collective-permute-start(bf16[288,1536]{1,0:T(8,128)(2,1)S(1)} %pack.3.refs_7_), channel_id=1, source_target_pairs={{0,1},{1,0},{2,3},{3,2},{4,5},{5,4},{6,7},{7,6},{8,9},{9,8},{10,11... | collective-permute-start | bytes 2654216 | tf_op jit(solution)/shard_map/ppermute | solution.py:30
  27.1 2.0 %collective-permute-start.4 = (bf16[192,1536]{1,0:T(8,128)(2,1)S(1)}, bf16[192,1536]{1,0:T(8,128)(2,1)S(1)}, u32[]{:S(2)}, u32[]{:S(2)}) collective-permute-start(bf16[192,1536]{1,0:T(8,128)(2,1)S(1)} %tie.5.refs_4_.refs_17_), channel_id=1, source_target_pairs={{0,2},{1,3},{2,0},{3,1},{4,6},{5,7},{6,4},{7,5},{8,10},{9,11},{10,... | collective-permute-start | bytes 1769480 | tf_op jit(solution)/shard_map/ppermute | solution.py:30
  31.7 14.9 %collective-permute-start.5 = (bf16[2,3,28,384]{3,2,1,0:T(8,128)(2,1)S(1)}, bf16[2,3,28,384]{3,2,1,0:T(8,128)(2,1)S(1)}, u32[]{:S(2)}, u32[]{:S(2)}) collective-permute-start(bf16[2,3,28,384]{3,2,1,0:T(8,128)(2,1)S(1)} %get-tuple-element.82), channel_id=1, source_target_pairs={{2,0},{3,1},{4,2},{5,3},{6,4},{7,5},{8,6},{9,7},{10,8},{11,9},{12,... | collective-permute-start | bytes 387080 | tf_op jit(solution)/shard_map/ppermute | solution.py:36
  36.6 10.0 %collective-permute-start.6 = (bf16[2,7,3,384]{3,2,1,0:T(4,128)(2,1)S(1)}, bf16[2,7,3,384]{3,2,1,0:T(4,128)(2,1)S(1)}, u32[]{:S(2)}, u32[]{:S(2)}) collective-permute-start(bf16[2,7,3,384]{3,2,1,0:T(4,128)(2,1)S(1)} %get-tuple-element.83), channel_id=1, source_target_pairs={{1,0},{0,1},{3,2},{2,3},{5,4},{4,5},{7,6},{6,7},{9,8},{8,9},{11,10... | collective-permute-start | bytes 96776 | tf_op jit(solution)/shard_map/ppermute | solution.py:36
  38.1 8.0 %collective-permute-start.7 = (bf16[2,3,3,384]{3,2,1,0:T(4,128)(2,1)S(1)}, bf16[2,3,3,384]{3,2,1,0:T(4,128)(2,1)S(1)}, u32[]{:S(2)}, u32[]{:S(2)}) collective-permute-start(bf16[2,3,3,384]{3,2,1,0:T(4,128)(2,1)S(1)} %get-tuple-element.84), channel_id=1, source_target_pairs={{3,0},{2,1},{5,2},{4,3},{7,4},{6,5},{9,6},{8,7},{11,8},{10,9},{13,... | collective-permute-start | bytes 41480 | tf_op jit(solution)/shard_map/ppermute | solution.py:36
  46.6 2.4 %collective-permute-start.9 = (bf16[288,1536]{1,0:T(8,128)(2,1)S(1)}, bf16[288,1536]{1,0:T(8,128)(2,1)S(1)}, u32[]{:S(2)}, u32[]{:S(2)}) collective-permute-start(bf16[288,1536]{1,0:T(8,128)(2,1)S(1)} %tie.6.refs_8_.refs_13_.refs_17_), channel_id=1, source_target_pairs={{0,2},{1,3},{2,0},{3,1},{4,6},{5,7},{6,4},{7,5},{8,10},{9,11},{10,... | collective-permute-start | bytes 2654216 | tf_op jit(solution)/shard_map/ppermute | solution.py:30
  64.2 10.2 %collective-permute-start.13 = (bf16[2,2,2,4,48,384]{5,4,3,2,1,0:T(8,128)(2,1)S(1)}, bf16[2,2,2,4,48,384]{5,4,3,2,1,0:T(8,128)(2,1)S(1)}, u32[]{:S(2)}, u32[]{:S(2)}) collective-permute-start(bf16[2,2,2,4,48,384]{5,4,3,2,1,0:T(8,128)(2,1)S(1)} %get-tuple-element.107), channel_id=1, source_target_pairs={{0,2},{1,3},{2,0},{3,1},{4,6},{5,7},{6,4},{7,5},{8,10},{9,11},{10,... | collective-permute-start | bytes 3538952 | tf_op jit(solution)/shard_map/ppermute | solution.py:30
  65.2 9.1 %collective-permute-start.14 = (bf16[2,2,1,4,48,384]{5,4,3,2,1,0:T(8,128)(2,1)S(1)}, bf16[2,2,1,4,48,384]{5,4,3,2,1,0:T(8,128)(2,1)S(1)}, u32[]{:S(2)}, u32[]{:S(2)}) collective-permute-start(bf16[2,2,1,4,48,384]{5,4,3,2,1,0:T(8,128)(2,1)S(1)} %get-tuple-element.108), channel_id=1, source_target_pairs={{0,2},{1,3},{2,0},{3,1},{4,6},{5,7},{6,4},{7,5},{8,10},{9,11},{10,... | collective-permute-start | bytes 1769480 | tf_op jit(solution)/shard_map/ppermute | solution.py:30
  65.7 8.7 %collective-permute-start.10 = (bf16[2,3,28,384]{3,2,1,0:T(8,128)(2,1)S(1)}, bf16[2,3,28,384]{3,2,1,0:T(8,128)(2,1)S(1)}, u32[]{:S(2)}, u32[]{:S(2)}) collective-permute-start(bf16[2,3,28,384]{3,2,1,0:T(8,128)(2,1)S(1)} %get-tuple-element.93), channel_id=1, source_target_pairs={{30,0},{31,1},{0,2},{1,3},{2,4},{3,5},{4,6},{5,7},{6,8},{7,9},{8,1... | collective-permute-start | bytes 387080 | tf_op jit(solution)/shard_map/ppermute | solution.py:36
  65.8 8.5 %collective-permute-start.11 = (bf16[2,7,3,384]{3,2,1,0:T(4,128)(2,1)S(1)}, bf16[2,7,3,384]{3,2,1,0:T(4,128)(2,1)S(1)}, u32[]{:S(2)}, u32[]{:S(2)}) collective-permute-start(bf16[2,7,3,384]{3,2,1,0:T(4,128)(2,1)S(1)} %get-tuple-element.94), channel_id=1, source_target_pairs={{1,0},{0,1},{3,2},{2,3},{5,4},{4,5},{7,6},{6,7},{9,8},{8,9},{11,10... | collective-permute-start | bytes 96776 | tf_op jit(solution)/shard_map/ppermute | solution.py:36
  67.6 6.8 %collective-permute-start.12 = (bf16[2,3,3,384]{3,2,1,0:T(4,128)(2,1)S(1)}, bf16[2,3,3,384]{3,2,1,0:T(4,128)(2,1)S(1)}, u32[]{:S(2)}, u32[]{:S(2)}) collective-permute-start(bf16[2,3,3,384]{3,2,1,0:T(4,128)(2,1)S(1)} %get-tuple-element.95), channel_id=1, source_target_pairs={{31,0},{30,1},{1,2},{0,3},{3,4},{2,5},{5,6},{4,7},{7,8},{6,9},{9,1... | collective-permute-start | bytes 41480 | tf_op jit(solution)/shard_map/ppermute | solution.py:36
  74.8 19.5 %collective-permute-start.15 = (bf16[2,3,4,48,384]{4,3,2,1,0:T(8,128)(2,1)S(1)}, bf16[2,3,4,48,384]{4,3,2,1,0:T(8,128)(2,1)S(1)}, u32[]{:S(2)}, u32[]{:S(2)}) collective-permute-start(bf16[2,3,4,48,384]{4,3,2,1,0:T(8,128)(2,1)S(1)} %get-tuple-element.115), channel_id=1, source_target_pairs={{0,1},{1,0},{2,3},{3,2},{4,5},{5,4},{6,7},{7,6},{8,9},{9,8},{10,11... | collective-permute-start | bytes 2654216 | tf_op jit(solution)/shard_map/ppermute | solution.py:30
  94.5 7.2 %collective-permute-start.16 = (bf16[2,2,3,4,48,384]{5,4,3,2,1,0:T(8,128)(2,1)S(1)}, bf16[2,2,3,4,48,384]{5,4,3,2,1,0:T(8,128)(2,1)S(1)}, u32[]{:S(2)}, u32[]{:S(2)}) collective-permute-start(bf16[2,2,3,4,48,384]{5,4,3,2,1,0:T(8,128)(2,1)S(1)} %tie.7), channel_id=1, source_target_pairs={{0,2},{1,3},{2,0},{3,1},{4,6},{5,7},{6,4},{7,5},{8,10},{9,11},{10,... | collective-permute-start | bytes 5308424 | tf_op jit(solution)/shard_map/ppermute | solution.py:30
  94.6 14.2 %collective-permute-start.25 = (bf16[288,384]{1,0:T(8,128)(2,1)S(1)}, bf16[288,384]{1,0:T(8,128)(2,1)S(1)}, u32[]{:S(2)}, u32[]{:S(2)}) collective-permute-start(bf16[288,384]{1,0:T(8,128)(2,1)S(1)} %get-tuple-element.129), channel_id=1, source_target_pairs={{0,12},{1,13},{2,14},{3,15},{4,8},{5,9},{6,10},{7,11},{8,4},{9,5},... | collective-permute-start | bytes 663560 | tf_op jit(solution)/shard_map/ppermute | solution.py:30
  96.9 11.9 %collective-permute-start.26 = (bf16[288,384]{1,0:T(8,128)(2,1)S(1)}, bf16[288,384]{1,0:T(8,128)(2,1)S(1)}, u32[]{:S(2)}, u32[]{:S(2)}) collective-permute-start(bf16[288,384]{1,0:T(8,128)(2,1)S(1)} %get-tuple-element.130), channel_id=1, source_target_pairs={{0,4},{1,5},{2,6},{3,7},{4,0},{5,1},{6,2},{7,3},{8,12},{9,13},{10,... | collective-permute-start | bytes 663560 | tf_op jit(solution)/shard_map/ppermute | solution.py:30
  97.7 11.1 %collective-permute-start.27 = (bf16[288,384]{1,0:T(8,128)(2,1)S(1)}, bf16[288,384]{1,0:T(8,128)(2,1)S(1)}, u32[]{:S(2)}, u32[]{:S(2)}) collective-permute-start(bf16[288,384]{1,0:T(8,128)(2,1)S(1)} %get-tuple-element.131), channel_id=1, source_target_pairs={{0,8},{1,9},{2,10},{3,11},{4,12},{5,13},{6,14},{7,15},{8,0},{9,1},... | collective-permute-start | bytes 663560 | tf_op jit(solution)/shard_map/ppermute | solution.py:30
  100.5 1.2 collective-permute-start.17
  102.2 16.7 %collective-permute-start.18 = (bf16[304,384]{1,0:T(8,128)(2,1)S(1)}, bf16[304,384]{1,0:T(8,128)(2,1)S(1)}, u32[]{:S(2)}, u32[]{:S(2)}) collective-permute-start(bf16[304,384]{1,0:T(8,128)(2,1)S(1)} %get-tuple-element.122), channel_id=1, source_target_pairs={{0,13},{1,12},{2,15},{3,14},{4,9},{5,8},{6,11},{7,10},{8,5},{9,4},... | collective-permute-start | bytes 700424 | tf_op jit(solution)/shard_map/ppermute | solution.py:30
  104.5 15.8 %collective-permute-start.19 = (bf16[304,384]{1,0:T(8,128)(2,1)S(1)}, bf16[304,384]{1,0:T(8,128)(2,1)S(1)}, u32[]{:S(2)}, u32[]{:S(2)}) collective-permute-start(bf16[304,384]{1,0:T(8,128)(2,1)S(1)} %get-tuple-element.123), channel_id=1, source_target_pairs={{0,5},{1,4},{2,7},{3,6},{4,1},{5,0},{6,3},{7,2},{8,13},{9,12},{10,... | collective-permute-start | bytes 700424 | tf_op jit(solution)/shard_map/ppermute | solution.py:30
  108.9 0.9 copy-start.12
  109.9 8.1 %collective-permute-start.28 = (bf16[144,384]{1,0:T(8,128)(2,1)S(1)}, bf16[144,384]{1,0:T(8,128)(2,1)S(1)}, u32[]{:S(2)}, u32[]{:S(2)}) collective-permute-start(bf16[144,384]{1,0:T(8,128)(2,1)S(1)} %get-tuple-element.133), channel_id=1, source_target_pairs={{0,16},{1,17},{2,18},{3,19},{4,20},{5,21},{6,22},{7,23},{8,24},{9,... | collective-permute-start | bytes 331784 | tf_op jit(solution)/shard_map/ppermute | solution.py:30
  112.6 11.6 %collective-permute-start.20 = (bf16[304,384]{1,0:T(8,128)(2,1)S(1)}, bf16[304,384]{1,0:T(8,128)(2,1)S(1)}, u32[]{:S(2)}, u32[]{:S(2)}) collective-permute-start(bf16[304,384]{1,0:T(8,128)(2,1)S(1)} %get-tuple-element.124), channel_id=1, source_target_pairs={{0,9},{1,8},{2,11},{3,10},{4,13},{5,12},{6,15},{7,14},{8,1},{9,0},... | collective-permute-start | bytes 700424 | tf_op jit(solution)/shard_map/ppermute | solution.py:30
  113.9 14.0 %collective-permute-start.21 = (bf16[304,384]{1,0:T(8,128)(2,1)S(1)}, bf16[304,384]{1,0:T(8,128)(2,1)S(1)}, u32[]{:S(2)}, u32[]{:S(2)}) collective-permute-start(bf16[304,384]{1,0:T(8,128)(2,1)S(1)} %get-tuple-element.125), channel_id=1, source_target_pairs={{0,1},{1,0},{2,3},{3,2},{4,5},{5,4},{6,7},{7,6},{8,9},{9,8},{10,11... | collective-permute-start | bytes 700424 | tf_op jit(solution)/shard_map/ppermute | solution.py:30
  118.0 11.6 %collective-permute-start.22 = (bf16[304,384]{1,0:T(8,128)(2,1)S(1)}, bf16[304,384]{1,0:T(8,128)(2,1)S(1)}, u32[]{:S(2)}, u32[]{:S(2)}) collective-permute-start(bf16[304,384]{1,0:T(8,128)(2,1)S(1)} %get-tuple-element.126), channel_id=1, source_target_pairs={{0,12},{1,13},{2,14},{3,15},{4,8},{5,9},{6,10},{7,11},{8,4},{9,5},... | collective-permute-start | bytes 700424 | tf_op jit(solution)/shard_map/ppermute | solution.py:30
  118.9 11.4 %collective-permute-start.23 = (bf16[304,384]{1,0:T(8,128)(2,1)S(1)}, bf16[304,384]{1,0:T(8,128)(2,1)S(1)}, u32[]{:S(2)}, u32[]{:S(2)}) collective-permute-start(bf16[304,384]{1,0:T(8,128)(2,1)S(1)} %get-tuple-element.127), channel_id=1, source_target_pairs={{0,4},{1,5},{2,6},{3,7},{4,0},{5,1},{6,2},{7,3},{8,12},{9,13},{10,... | collective-permute-start | bytes 700424 | tf_op jit(solution)/shard_map/ppermute | solution.py:30
  120.2 12.8 %collective-permute-start.24 = (bf16[304,384]{1,0:T(8,128)(2,1)S(1)}, bf16[304,384]{1,0:T(8,128)(2,1)S(1)}, u32[]{:S(2)}, u32[]{:S(2)}) collective-permute-start(bf16[304,384]{1,0:T(8,128)(2,1)S(1)} %get-tuple-element.128), channel_id=1, source_target_pairs={{0,8},{1,9},{2,10},{3,11},{4,12},{5,13},{6,14},{7,15},{8,0},{9,1},... | collective-permute-start | bytes 700424 | tf_op jit(solution)/shard_map/ppermute | solution.py:30
  133.3 17.0 %collective-permute-start.29 = (bf16[160,384]{1,0:T(8,128)(2,1)S(1)}, bf16[160,384]{1,0:T(8,128)(2,1)S(1)}, u32[]{:S(2)}, u32[]{:S(2)}) collective-permute-start(bf16[160,384]{1,0:T(8,128)(2,1)S(1)} %get-tuple-element.135), channel_id=1, source_target_pairs={{0,16},{1,17},{2,18},{3,19},{4,20},{5,21},{6,22},{7,23},{8,24},{9,... | collective-permute-start | bytes 368648 | tf_op jit(solution)/shard_map/ppermute | solution.py:30
  136.1 10.5 %collective-permute-start.31 = (bf16[144,384]{1,0:T(8,128)(2,1)S(1)}, bf16[144,384]{1,0:T(8,128)(2,1)S(1)}, u32[]{:S(2)}, u32[]{:S(2)}) collective-permute-start(bf16[144,384]{1,0:T(8,128)(2,1)S(1)} %add_convert_fusion.1.refs_8_.refs_0_), channel_id=1, source_target_pairs={{0,16},{1,17},{2,18},{3,19},{4,20},{5,21},{6,22},{7,23},{8,24},{9,... | collective-permute-start | bytes 331784 | tf_op jit(solution)/shard_map/ppermute | solution.py:30
  146.7 17.2 %collective-permute-start.42 = (bf16[2,144,384]{2,1,0:T(8,128)(2,1)S(1)}, bf16[2,144,384]{2,1,0:T(8,128)(2,1)S(1)}, u32[]{:S(2)}, u32[]{:S(2)}) collective-permute-start(bf16[2,144,384]{2,1,0:T(8,128)(2,1)S(1)} %stack.2.refs_2_.refs_0_), channel_id=1, source_target_pairs={{0,2},{1,3},{2,0},{3,1},{4,6},{5,7},{6,4},{7,5},{8,10},{9,11},{10,... | collective-permute-start | bytes 663560 | tf_op jit(solution)/shard_map/ppermute | solution.py:30
  146.8 11.9 %collective-permute-start.41 = (bf16[2,144,384]{2,1,0:T(8,128)(2,1)S(1)}, bf16[2,144,384]{2,1,0:T(8,128)(2,1)S(1)}, u32[]{:S(2)}, u32[]{:S(2)}) collective-permute-start(bf16[2,144,384]{2,1,0:T(8,128)(2,1)S(1)} %stack.2.refs_2_.refs_0_), channel_id=1, source_target_pairs={{0,12},{1,13},{2,14},{3,15},{4,8},{5,9},{6,10},{7,11},{8,4},{9,5},... | collective-permute-start | bytes 663560 | tf_op jit(solution)/shard_map/ppermute | solution.py:30
  147.0 12.4 %collective-permute-start.40 = (bf16[2,144,384]{2,1,0:T(8,128)(2,1)S(1)}, bf16[2,144,384]{2,1,0:T(8,128)(2,1)S(1)}, u32[]{:S(2)}, u32[]{:S(2)}) collective-permute-start(bf16[2,144,384]{2,1,0:T(8,128)(2,1)S(1)} %stack.2.refs_2_.refs_0_), channel_id=1, source_target_pairs={{0,4},{1,5},{2,6},{3,7},{4,0},{5,1},{6,2},{7,3},{8,12},{9,13},{10,... | collective-permute-start | bytes 663560 | tf_op jit(solution)/shard_map/ppermute | solution.py:30
  148.7 16.9 %collective-permute-start.39 = (bf16[2,144,384]{2,1,0:T(8,128)(2,1)S(1)}, bf16[2,144,384]{2,1,0:T(8,128)(2,1)S(1)}, u32[]{:S(2)}, u32[]{:S(2)}) collective-permute-start(bf16[2,144,384]{2,1,0:T(8,128)(2,1)S(1)} %stack.2.refs_2_.refs_0_), channel_id=1, source_target_pairs={{0,8},{1,9},{2,10},{3,11},{4,12},{5,13},{6,14},{7,15},{8,0},{9,1},... | collective-permute-start | bytes 663560 | tf_op jit(solution)/shard_map/ppermute | solution.py:30
  150.4 9.5 %collective-permute-start.30 = (bf16[160,384]{1,0:T(8,128)(2,1)S(1)}, bf16[160,384]{1,0:T(8,128)(2,1)S(1)}, u32[]{:S(2)}, u32[]{:S(2)}) collective-permute-start(bf16[160,384]{1,0:T(8,128)(2,1)S(1)} %add_convert_fusion.refs_0_), channel_id=1, source_target_pairs={{0,16},{1,17},{2,18},{3,19},{4,20},{5,21},{6,22},{7,23},{8,24},{9,... | collective-permute-start | bytes 368648 | tf_op jit(solution)/shard_map/ppermute | solution.py:30
  158.7 6.9 %collective-permute-start.45 = (bf16[2,144,384]{2,1,0:T(8,128)(2,1)S(1)}, bf16[2,144,384]{2,1,0:T(8,128)(2,1)S(1)}, u32[]{:S(2)}, u32[]{:S(2)}) collective-permute-start(bf16[2,144,384]{2,1,0:T(8,128)(2,1)S(1)} %collective-permute-done.41.refs_3_), channel_id=1, source_target_pairs={{0,2},{1,3},{2,0},{3,1},{4,6},{5,7},{6,4},{7,5},{8,10},{9,11},{10,... | collective-permute-start | bytes 663560 | tf_op jit(solution)/shard_map/ppermute | solution.py:30
  159.3 7.0 %collective-permute-start.44 = (bf16[2,144,384]{2,1,0:T(8,128)(2,1)S(1)}, bf16[2,144,384]{2,1,0:T(8,128)(2,1)S(1)}, u32[]{:S(2)}, u32[]{:S(2)}) collective-permute-start(bf16[2,144,384]{2,1,0:T(8,128)(2,1)S(1)} %collective-permute-done.40.refs_2_), channel_id=1, source_target_pairs={{0,2},{1,3},{2,0},{3,1},{4,6},{5,7},{6,4},{7,5},{8,10},{9,11},{10,... | collective-permute-start | bytes 663560 | tf_op jit(solution)/shard_map/ppermute | solution.py:30
  159.8 10.4 %collective-permute-start.34 = (bf16[2,144,384]{2,1,0:T(8,128)(2,1)S(1)}, bf16[2,144,384]{2,1,0:T(8,128)(2,1)}, u32[]{:S(2)}, u32[]{:S(2)}) collective-permute-start(bf16[2,144,384]{2,1,0:T(8,128)(2,1)S(1)} %stack.3.refs_0_), channel_id=1, source_target_pairs={{0,12},{1,13},{2,14},{3,15},{4,8},{5,9},{6,10},{7,11},{8,4},{9,5},... | collective-permute-start | bytes 663560 | tf_op jit(solution)/shard_map/ppermute | solution.py:30
  163.9 10.3 %collective-permute-start.33 = (bf16[2,144,384]{2,1,0:T(8,128)(2,1)S(1)}, bf16[2,144,384]{2,1,0:T(8,128)(2,1)}, u32[]{:S(2)}, u32[]{:S(2)}) collective-permute-start(bf16[2,144,384]{2,1,0:T(8,128)(2,1)S(1)} %stack.3.refs_0_), channel_id=1, source_target_pairs={{0,4},{1,5},{2,6},{3,7},{4,0},{5,1},{6,2},{7,3},{8,12},{9,13},{10,... | collective-permute-start | bytes 663560 | tf_op jit(solution)/shard_map/ppermute | solution.py:30
  165.6 8.9 %collective-permute-start.32 = (bf16[2,144,384]{2,1,0:T(8,128)(2,1)S(1)}, bf16[2,144,384]{2,1,0:T(8,128)(2,1)}, u32[]{:S(2)}, u32[]{:S(2)}) collective-permute-start(bf16[2,144,384]{2,1,0:T(8,128)(2,1)S(1)} %stack.3.refs_0_), channel_id=1, source_target_pairs={{0,8},{1,9},{2,10},{3,11},{4,12},{5,13},{6,14},{7,15},{8,0},{9,1},... | collective-permute-start | bytes 663560 | tf_op jit(solution)/shard_map/ppermute | solution.py:30
  165.6 0.7 copy-start.8
  166.3 9.1 %collective-permute-start.43 = (bf16[2,144,384]{2,1,0:T(8,128)(2,1)S(1)}, bf16[2,144,384]{2,1,0:T(8,128)(2,1)}, u32[]{:S(2)}, u32[]{:S(2)}) collective-permute-start(bf16[2,144,384]{2,1,0:T(8,128)(2,1)S(1)} %collective-permute-done.39.refs_1_), channel_id=1, source_target_pairs={{0,2},{1,3},{2,0},{3,1},{4,6},{5,7},{6,4},{7,5},{8,10},{9,11},{10,... | collective-permute-start | bytes 663560 | tf_op jit(solution)/shard_map/ppermute | solution.py:30
  166.3 0.7 copy-start.10
  167.0 13.4 %collective-permute-start.35 = (bf16[2,144,384]{2,1,0:T(8,128)(2,1)S(1)}, bf16[2,144,384]{2,1,0:T(8,128)(2,1)}, u32[]{:S(2)}, u32[]{:S(2)}) collective-permute-start(bf16[2,144,384]{2,1,0:T(8,128)(2,1)S(1)} %stack.3.refs_0_), channel_id=1, source_target_pairs={{0,2},{1,3},{2,0},{3,1},{4,6},{5,7},{6,4},{7,5},{8,10},{9,11},{10,... | collective-permute-start | bytes 663560 | tf_op jit(solution)/shard_map/ppermute | solution.py:30
  170.3 10.2 %collective-permute-start.38 = (bf16[2,144,384]{2,1,0:T(8,128)(2,1)}, bf16[2,144,384]{2,1,0:T(8,128)(2,1)}, u32[]{:S(2)}, u32[]{:S(2)}) collective-permute-start(bf16[2,144,384]{2,1,0:T(8,128)(2,1)} %collective-permute-done.34.refs_3_), channel_id=1, source_target_pairs={{0,2},{1,3},{2,0},{3,1},{4,6},{5,7},{6,4},{7,5},{8,10},{9,11},{10,... | collective-permute-start | bytes 663560 | tf_op jit(solution)/shard_map/ppermute | solution.py:30
  174.2 6.3 %collective-permute-start.37 = (bf16[2,144,384]{2,1,0:T(8,128)(2,1)}, bf16[2,144,384]{2,1,0:T(8,128)(2,1)}, u32[]{:S(2)}, u32[]{:S(2)}) collective-permute-start(bf16[2,144,384]{2,1,0:T(8,128)(2,1)} %collective-permute-done.33.refs_2_), channel_id=1, source_target_pairs={{0,2},{1,3},{2,0},{3,1},{4,6},{5,7},{6,4},{7,5},{8,10},{9,11},{10,... | collective-permute-start | bytes 663560 | tf_op jit(solution)/shard_map/ppermute | solution.py:30
  174.5 6.0 %collective-permute-start.36 = (bf16[2,144,384]{2,1,0:T(8,128)(2,1)}, bf16[2,144,384]{2,1,0:T(8,128)(2,1)}, u32[]{:S(2)}, u32[]{:S(2)}) collective-permute-start(bf16[2,144,384]{2,1,0:T(8,128)(2,1)} %collective-permute-done.32.refs_1_), channel_id=1, source_target_pairs={{0,2},{1,3},{2,0},{3,1},{4,6},{5,7},{6,4},{7,5},{8,10},{9,11},{10,... | collective-permute-start | bytes 663560 | tf_op jit(solution)/shard_map/ppermute | solution.py:30
  175.4 0.9 copy-start.9
  176.3 0.9 copy-start.11
